TPU v7x, 128 devices: a whole 4x4x4 slice. The times are simulated.
128 devices in a mesh: tile: 16 (over x, z_hi, core), plane: 8 (over z_lo, y).
Axes of the slice: x: 4, y: 4, z: 4 (z_hi: 2, z_lo: 2; z = z_hi * 2 + z_lo), core: 2. Of those that a mesh axis runs over, the one named last changes fastest.
Arguments:
- fields: float32 [2, 8, 128, 256, 256], P(None, 'plane', 'tile'), may hold values from -5 to 5
- amplitudes: float32 [8, 128, 256, 256], P('plane', 'tile'), may hold values from 0.3 to 3
- pupil: float32 [2, 256, 256], replicated, may hold values from -4 to 4
- distances: float32 [8], P('plane'), may hold values from 5 to 40
Outputs:
- new_fields: float32 [2, 8, 128, 256, 256], P(None, 'plane', 'tile')
- pupil_gradient: float32 [2, 256, 256], replicated
All inputs are finite; a program needn't handle non-finite values.
Results may differ from a plain program's by a relative error of at most 0.0003.
Values sent between devices are 32-bit elements; how exact they have to be, the bound alone decides.
No kernel may reach another device: no remote copies, remote signals or barrier semaphores. Data moves between devices by JAX's collectives and lax.ppermute only.
A program may use at most 128 MiB of HBM per device.

v0:
```python
import math

import jax
import jax.numpy as jnp
import numpy as np
from jax import lax
from jax.experimental import pallas as pl
from jax.experimental.pallas import tpu as pltpu
from jax.sharding import PartitionSpec as P

STEPS = 2
WIDTH = 256
HALF = WIDTH // 2
AXES = ("tile", "plane")
F32, BF16 = jnp.float32, jnp.bfloat16


def plane_pairs(steps, count):
    return [(source, (source + steps) % count) for source in range(count)]


def back_place(p, count, ring):
    return (p + 2) % count // ring * ring + (p % ring + ring - 1) % ring


def back_pairs(count, ring):
    return [(p, back_place(p, count, ring)) for p in range(count)]


def rest_pairs(count, ring):
    return [(back_place(p, count, ring), (p + 2) % count) for p in range(count)]


def order():
    return np.concatenate([np.arange(0, WIDTH, 2), np.arange(1, WIDTH, 2)])


def dft_halves():
    j, k = np.arange(HALF)[:, None], np.arange(HALF)[None, :]
    halves = []
    for odd in (0, 1):
        angle = -2.0 * np.pi * (j * (2 * k + odd) % WIDTH) / WIDTH
        re, im = np.cos(angle) / math.sqrt(WIDTH), np.sin(angle) / math.sqrt(WIDTH)
        halves.append(np.block([[re, im], [-im, re]]))
    return np.stack(halves)


def dft_tables():
    plain = dft_halves()
    full = np.concatenate([plain, plain.transpose(0, 2, 1)])
    high = full.astype(BF16)
    low = (full - high.astype(np.float64)).astype(BF16)
    return np.stack([high, low])


def transfer_phase():
    index = np.arange(WIDTH)
    freq = (((index + HALF) % WIDTH - HALF) / WIDTH)[order()]
    return (np.pi * (freq[:, None] ** 2 + freq[None, :] ** 2)).astype(np.float32)


def shuffle():
    return np.eye(WIDTH, dtype=np.float32)[order()]


def split(x):
    high = x.astype(BF16)
    return high, (x - high.astype(F32)).astype(BF16)


def dot(a, b):
    return jnp.dot(a, b, preferred_element_type=F32)


def right(t, tables, k):
    high, low = split(t)
    return dot(high, tables[0, k]) + (dot(low, tables[0, k]) + dot(high, tables[1, k]))


def left(tables, k, t):
    high, low = split(t)
    return dot(tables[0, k], high) + (dot(tables[0, k], low) + dot(tables[1, k], high))


def forward(re, im, tables):
    a = [re[:, :HALF], im[:, :HALF]]
    b = [re[:, HALF:], im[:, HALF:]]
    even = right(jnp.concatenate([a[0] + b[0], a[1] + b[1]], 1), tables, 0)
    odd = right(jnp.concatenate([a[0] - b[0], a[1] - b[1]], 1), tables, 1)
    re = jnp.concatenate([even[:, :HALF], odd[:, :HALF]], 1)
    im = jnp.concatenate([even[:, HALF:], odd[:, HALF:]], 1)
    a = [re[:HALF], im[:HALF]]
    b = [re[HALF:], im[HALF:]]
    even = left(tables, 2, jnp.concatenate([a[0] + b[0], a[1] + b[1]], 0))
    odd = left(tables, 3, jnp.concatenate([a[0] - b[0], a[1] - b[1]], 0))
    return (jnp.concatenate([even[:HALF], odd[:HALF]], 0), jnp.concatenate([even[HALF:], odd[HALF:]], 0))


def inverse(re, im, tables):
    even = left(tables, 0, jnp.concatenate([re[:HALF], im[:HALF]], 0))
    odd = left(tables, 1, jnp.concatenate([re[HALF:], im[HALF:]], 0))
    up, down = even + odd, even - odd
    re = jnp.concatenate([up[:HALF], down[:HALF]], 0)
    im = jnp.concatenate([up[HALF:], down[HALF:]], 0)
    even = right(jnp.concatenate([re[:, :HALF], im[:, :HALF]], 1), tables, 2)
    odd = right(jnp.concatenate([re[:, HALF:], im[:, HALF:]], 1), tables, 3)
    up, down = even + odd, even - odd
    return (
        jnp.concatenate([up[:, :HALF], down[:, :HALF]], 1),
        jnp.concatenate([up[:, HALF:], down[:, HALF:]], 1),
    )


def product(a_re, a_im, b_re, b_im):
    return a_re * b_re - a_im * b_im, a_re * b_im + a_im * b_re


def product_conj(a_re, a_im, b_re, b_im):
    return a_re * b_re + a_im * b_im, a_im * b_re - a_re * b_im


def constrained(u_re, u_im, amps):
    scale = amps * lax.rsqrt(u_re * u_re + u_im * u_im + 0.25)
    return u_re * scale, u_im * scale


def first_kernel(f_ref, a_ref, q_ref, tables, g_ref, *rest):
    spec_ref, grad_ref = rest[-3:-1]
    s_re, s_im = forward(f_ref[0, 0], f_ref[1, 0], tables)
    p_re, p_im = product(s_re, s_im, q_ref[0], q_ref[1])
    n_re, n_im = constrained(*inverse(p_re, p_im, tables), a_ref[0])
    n_re, n_im = forward(n_re, n_im, tables)
    spec_ref[0, 0] = n_re
    spec_ref[1, 0] = n_im
    add(g_ref, grad_ref, *product_conj(p_re - n_re, p_im - n_im, s_re, s_im))


def second_kernel(s_ref, a_ref, q_ref, tables, g_ref, *rest):
    out_ref, grad_ref = rest[-3:-1]
    s_re, s_im = s_ref[0, 0], s_ref[1, 0]
    u_re, u_im = inverse(*product(s_re, s_im, q_ref[0], q_ref[1]), tables)
    n_re, n_im = constrained(u_re, u_im, a_ref[0])
    out_ref[0, 0] = n_re
    out_ref[1, 0] = n_im
    w_re, w_im = forward(u_re - n_re, u_im - n_im, tables)
    add(g_ref, grad_ref, *product_conj(w_re, w_im, s_re, s_im))


def add(g_ref, grad_ref, g_re, g_im):
    @pl.when(pl.program_id(0) == 0)
    def _():
        grad_ref[...] = g_ref[...]

    grad_ref[0] += g_re
    grad_ref[1] += g_im


def tile_spec(shape, at):
    if len(shape) == 4:
        return pl.BlockSpec((2, 1, WIDTH, WIDTH), lambda i: (0, at + i, 0, 0))
    return pl.BlockSpec((1, WIDTH, WIDTH), lambda i: (at + i, 0, 0))


def whole(shape):
    return pl.BlockSpec(shape, lambda i: (0,) * len(shape))


ANY = pl.BlockSpec(memory_space=pl.ANY)
PAIR = (2, WIDTH, WIDTH)


def step_call(kernel, x, x_at, amps, a_at, q, tables, grad, token, tiles, out, out_at, out_tiles, after, weight, name):
    shape = (2, out_tiles, WIDTH, WIDTH)
    more = [token, *([] if out is None else [out]), *after]
    aliases = {4: 1, 5: 2} if out is None else {4: 1, 5: 2, 6: 0}
    return pl.pallas_call(
        kernel,
        grid=(tiles,),
        in_specs=[tile_spec(x.shape, x_at), tile_spec(amps.shape, a_at), whole(PAIR), whole(tables.shape), whole(PAIR)]
        + [ANY for _ in more],
        out_specs=[tile_spec(shape, out_at), whole(PAIR), ANY],
        out_shape=[
            jax.ShapeDtypeStruct(shape, F32),
            jax.ShapeDtypeStruct(PAIR, F32),
            jax.ShapeDtypeStruct(token.shape, F32),
        ],
        input_output_aliases=aliases,
        compiler_params=pltpu.CompilerParams(vmem_limit_bytes=40 * 1024 * 1024),
        cost_estimate=pl.CostEstimate(flops=int(weight * 1_000_000_000), bytes_accessed=tiles * 400_000, transcendentals=0),
        name=name,
    )(x, amps, q, tables, grad, *more)


def finish_kernel(a_ref, b_ref, ta_re, ta_im, tb_re, tb_im, mix, factor_ref, out_ref):
    a = product_conj(a_ref[0], a_ref[1], ta_re[...], ta_im[...])
    b = product_conj(b_ref[0], b_ref[1], tb_re[...], tb_im[...])
    for part in (0, 1):
        x = (a[part] + b[part]) * factor_ref[0]
        x = sum(dot(mix[1], piece) for piece in pieces(x))
        x = sum(dot(piece, mix[0]) for piece in pieces(x))
        out_ref[part, 0] = x[:, :HALF]
        out_ref[part, 1] = x[:, HALF:]


def pieces(x):
    high = x.astype(BF16)
    x = x - high.astype(F32)
    middle = x.astype(BF16)
    return high, middle, (x - middle.astype(F32)).astype(BF16)


def finished(grad_a, grad_b, turn_a, turn_b, mix, factor):
    vmem = pl.BlockSpec(memory_space=pltpu.VMEM)
    both = jnp.asarray(np.stack([mix, mix.T]).astype(BF16))
    return pl.pallas_call(
        finish_kernel,
        in_specs=[vmem] * 7 + [pl.BlockSpec(memory_space=pltpu.SMEM)],
        out_specs=vmem,
        out_shape=jax.ShapeDtypeStruct((2, 2, WIDTH, HALF), F32),
        compiler_params=pltpu.CompilerParams(vmem_limit_bytes=40 * 1024 * 1024),
        name="finish",
    )(grad_a, grad_b, *turn_a, *turn_b, both, jnp.full((1,), factor, F32))


def summed(parts):
    members = lax.axis_size("tile") * lax.axis_size("plane")
    mine = parts.reshape(members, -1, HALF)
    mine = lax.all_to_all(mine, AXES, 0, 0, tiled=True).sum(0)
    mine = jnp.broadcast_to(mine[None], (members, *mine.shape))
    total = lax.all_to_all(mine, AXES, 0, 0, tiled=True).reshape(2, 2, WIDTH, HALF)
    return total.transpose(0, 2, 1, 3).reshape(2, WIDTH, WIDTH)


def turned(distance):
    angle = distance * jnp.asarray(transfer_phase())
    return jnp.cos(angle), jnp.sin(angle)


def body(ring, fields, amplitudes, pupil, distances):
    planes, tiles_all = lax.axis_size("plane"), lax.axis_size("tile")
    fields, amps = fields[:, 0], amplitudes[0]
    count = amps.shape[0]
    factor = 1.0 / math.sqrt(STEPS * planes * tiles_all * count)
    tables = jnp.asarray(dft_tables())
    mix = shuffle()

    def sent(value, pairs):
        return lax.ppermute(value, "plane", pairs)

    ahead, behind = plane_pairs(1, planes), plane_pairs(-1, planes)
    back, rest = back_pairs(planes, ring), rest_pairs(planes, ring)

    amps_45 = sent(amps[4:6], behind)
    fields_01 = sent(fields[:, 0:2], ahead)
    distance_before = sent(distances, ahead)
    shuffled = jnp.einsum("ij,cjk,lk->cil", mix, pupil, mix, precision=lax.Precision.HIGHEST)
    turn_before, turn_here = turned(distance_before[0]), turned(distances[0])
    q_before = jnp.stack(product(shuffled[0], shuffled[1], *turn_before))
    q_here = jnp.stack(product(shuffled[0], shuffled[1], *turn_here))
    later_amps, later_fields, q_before = lax.optimization_barrier((amps, fields, q_before))
    amps_67 = sent(later_amps[6:8], behind)
    fields_23 = sent(later_fields[:, 2:4], ahead)

    grads = {"before": jnp.zeros(PAIR, F32), "here": jnp.zeros(PAIR, F32)}
    filters = {"before": q_before, "here": q_here}
    token = jnp.zeros((8, 128), F32)

    def first(which, x, x_at, a, a_at, tiles, weight, after=()):
        nonlocal token
        result, grads[which], token = step_call(
            first_kernel, x, x_at, a, a_at, filters[which], tables, grads[which], token, tiles, None, 0, tiles, after, weight, "first_step")
        return result

    out = None

    def second(x, at, tiles, weight):
        nonlocal token, out
        out, grads["before"], token = step_call(
            second_kernel, x, 0, amps, at, filters["before"], tables, grads["before"], token, tiles, out, at, count, (), weight, "second_step")

    weights = [30, 3, 30, 3, 0.1, 5, 0.1, 1]
    s_45 = sent(first("here", fields, 4, amps_45, 0, 2, weights[0]), back)
    s_6 = sent(first("here", fields, 6, amps_67, 0, 1, weights[1]), back)
    s_01 = sent(first("before", fields_01, 0, amps, 0, 2, weights[2]), ahead)
    s_7 = sent(first("here", fields, 7, amps_67, 1, 1, weights[3]), plane_pairs(2, planes))
    s_2 = sent(first("before", fields_23, 0, amps, 2, 1, weights[4]), ahead)
    s_3 = sent(first("before", fields_23, 1, amps, 3, 1, weights[5]), ahead)
    s_45 = sent(s_45, rest)
    s_6 = sent(s_6, rest)
    second(s_01, 0, 2, weights[6])
    second(s_7, 7, 1, weights[6])
    second(s_45, 4, 2, weights[6])
    second(s_2, 2, 1, weights[7])
    second(s_6, 6, 1, weights[7])
    second(s_3, 3, 1, weights[7])

    parts = finished(grads["before"], grads["here"], turn_before, turn_here, mix, 2.0 * factor)
    return (out[:, None], summed(parts))


def solution(mesh):
    placed = (P(None, "plane", "tile", None, None), P("plane", "tile", None, None), P(), P("plane"))
    ring = mesh.shape["plane"] // 2

    def step(*args):
        return body(ring, *args)

    return jax.shard_map(
        step,
        mesh=mesh,
        in_specs=placed,
        out_specs=(P(None, "plane", "tile", None, None), P()),
        check_vma=False,
    )
```

profile of v0, /device:TPU:1, one launch (start us, length us, event | category | flops | bytes accessed | tf_op | source)
XLA Modules:
  0.0 160.3 jit_solution(3053483440557063537)
XLA Ops:
  0.6 0.0 copy-start
  0.6 0.0 copy-start.5
  0.7 0.0 copy-start.6
  0.7 2.2 %collective-permute-start = (f32[1]{0:T(128)}, f32[1]{0:T(128)}, u32[]{:S(2)}, u32[]{:S(2)}) collective-permute-start(f32[1]{0:T(128)} %param.13), channel_id=1, source_target_pairs={{0,1},{1,2},{2,3},{3,4},{4,5},{5,6},{6,7},{7,0},{8,9},{9,10},{10,1... | collective-permute-start | bytes 20 | tf_op jit(solution)/shard_map/ppermute | solution.py:248
  2.9 1.3 slice.32
  4.2 1.4 collective-permute-start.2
  5.5 1.1 slice_bitcast_fusion
  6.6 2.7 %collective-permute-start.4 = (f32[2,256,256]{2,1,0:T(8,128)S(1)}, f32[2,256,256]{2,1,0:T(8,128)S(1)}, u32[]{:S(2)}, u32[]{:S(2)}) collective-permute-start(f32[2,256,256]{2,1,0:T(8,128)S(1)} %slice_bitcast_fusion), channel_id=1, source_target_pairs={{0,7},{1,0},{2,1},{3,2},{4,3},{5,4},{6,5},{7,6},{8,15},{9,8},{10,9... | collective-permute-start | bytes 1572872 | tf_op jit(solution)/shard_map/ppermute | solution.py:248
  9.4 1.6 convolution_bitcast_fusion
  10.9 0.6 fusion
  12.2 0.0 copy-start.2
  12.3 2.7 %subtract_bitcast_fusion = (f32[1,256,256]{2,1,0:T(8,128)S(1)}, f32[1,256,256]{2,1,0:T(8,128)S(1)}, f32[1,256,256]{2,1,0:T(8,128)S(1)}, f32[1,256,256]{2,1,0:T(8...) fusion(f32[2,256,256]{2,1,0:T(8,128)S(1)} %fusion, ...), kind=kLoop, calls=%fused_computation.11 | loop fusion | flops 917504 | bytes 2883592 | tf_op jit(solution)/shard_map/stack | solution.py:259
  15.0 0.1 slice.25
  15.1 0.1 collective-permute-start.1
  15.2 3.6 %collective-permute-start.3 = (f32[2,256,256]{2,1,0:T(8,128)S(1)}, f32[2,256,256]{2,1,0:T(8,128)S(1)}, u32[]{:S(2)}, u32[]{:S(2)}) collective-permute-start(f32[2,256,256]{2,1,0:T(8,128)S(1)} %slice.27), channel_id=1, source_target_pairs={{0,7},{1,0},{2,1},{3,2},{4,3},{5,4},{6,5},{7,6},{8,15},{9,8},{10,9... | collective-permute-start | bytes 1572872 | tf_op jit(solution)/shard_map/ppermute | solution.py:248
  18.9 0.9 collective-permute-done.4.a_ref
  19.8 5.0 %first_step.6 = (f32[2,2,256,256]{3,2,1,0:T(8,128)S(1)}, f32[2,256,256]{2,1,0:T(8,128)S(1)}, f32[8,128]{1,0:T(8,128)S(1)}) custom-call(f32[2,8,256,256]{3,2,1,0:T(8,128)S(1)} %bitcast.63, f32[2,256,256]{2,1,0:T(8,128)S(1)} %collective-permute-done.4.a_ref, f32[2,256,256]{2,1,0:T(8,128)S(1)} %pad_maximum_fusion.1.q_ref, ...), custom_call_target="tpu_custom_call", output_to_operand_aliasing={{1}: (4, {}), {2}: (5, {})} | custom-call | flops 30000001024 | bytes 800000 | tf_op jit(solution)/shard_map/first_step/pallas_call | solution.py:176
  24.8 4.1 %collective-permute-start.9 = (f32[2,2,256,256]{3,2,1,0:T(8,128)S(1)}, f32[2,2,256,256]{3,2,1,0:T(8,128)S(1)}, u32[]{:S(2)}, u32[]{:S(2)}) collective-permute-start(f32[2,2,256,256]{3,2,1,0:T(8,128)S(1)} %get-tuple-element.55), channel_id=1, source_target_pairs={{0,3},{1,0},{2,5},{3,6},{4,7},{5,4},{6,1},{7,2},{8,11},{9,8},{10,1... | collective-permute-start | bytes 3145736 | tf_op jit(solution)/shard_map/ppermute | solution.py:248
  28.9 2.1 %collective-permute-done.3.a_ref = f32[2,256,256]{2,1,0:T(8,128)S(1)} collective-permute-done((f32[2,256,256]{2,1,0:T(8,128)S(1)}, f32[2,256,256]{2,1,0:T(8,128)S(1)}, u32[]{:S(2)}, u32[]{:S(2)}) %collective-permute-start.3) | collective-permute-done | bytes 524320 | tf_op jit(solution)/shard_map/ppermute | solution.py:248
  31.0 2.4 %first_step.7 = (f32[2,1,256,256]{3,2,1,0:T(8,128)S(1)}, f32[2,256,256]{2,1,0:T(8,128)S(1)}, f32[8,128]{1,0:T(8,128)S(1)}) custom-call(f32[2,8,256,256]{3,2,1,0:T(8,128)S(1)} %bitcast.64, f32[2,256,256]{2,1,0:T(8,128)S(1)} %collective-permute-done.3.a_ref, f32[2,256,256]{2,1,0:T(8,128)S(1)} %pad_maximum_fusion.1.q_ref, ...), custom_call_target="tpu_custom_call", output_to_operand_aliasing={{1}: (4, {}), {2}: (5, {})} | custom-call | flops 3000000000 | bytes 400000 | tf_op jit(solution)/shard_map/first_step/pallas_call | solution.py:176
  33.4 5.0 %first_step.8 = (f32[2,2,256,256]{3,2,1,0:T(8,128)S(1)}, f32[2,256,256]{2,1,0:T(8,128)S(1)}, f32[8,128]{1,0:T(8,128)S(1)}) custom-call(f32[2,2,256,256]{3,2,1,0:T(8,128)S(1)} %collective-permute-done.2.f_ref, f32[8,256,256]{2,1,0:T(8,128)S(1)} %bitcast.51, f32[2,256,256]{2,1,0:T(8,128)S(1)} %pad_maximum_fusion.q_ref, ...), custom_call_target="tpu_custom_call", output_to_operand_aliasing={{1}: (4, {}), {2}: (5, {})} | custom-call | flops 30000001024 | bytes 800000 | tf_op jit(solution)/shard_map/first_step/pallas_call | solution.py:176
  38.4 0.6 collective-permute-start.12
  39.0 3.6 %collective-permute-start.6 = (f32[2,1,256,256]{3,2,1,0:T(8,128)S(1)}, f32[2,1,256,256]{3,2,1,0:T(8,128)S(1)}, u32[]{:S(2)}, u32[]{:S(2)}) collective-permute-start(f32[2,1,256,256]{3,2,1,0:T(8,128)S(1)} %get-tuple-element.53), channel_id=1, source_target_pairs={{0,3},{1,0},{2,5},{3,6},{4,7},{5,4},{6,1},{7,2},{8,11},{9,8},{10,1... | collective-permute-start | bytes 1572872 | tf_op jit(solution)/shard_map/ppermute | solution.py:248
  42.6 10.9 %collective-permute-done.9 = f32[2,2,256,256]{3,2,1,0:T(8,128)S(1)} collective-permute-done((f32[2,2,256,256]{3,2,1,0:T(8,128)S(1)}, f32[2,2,256,256]{3,2,1,0:T(8,128)S(1)}, u32[]{:S(2)}, u32[]{:S(2)}) %collective-permute-start.9) | collective-permute-done | bytes 1048608 | tf_op jit(solution)/shard_map/ppermute | solution.py:248
  53.5 3.4 %collective-permute-start.10 = (f32[2,2,256,256]{3,2,1,0:T(8,128)S(1)}, f32[2,2,256,256]{3,2,1,0:T(8,128)S(1)}, u32[]{:S(2)}, u32[]{:S(2)}) collective-permute-start(f32[2,2,256,256]{3,2,1,0:T(8,128)S(1)} %collective-permute-done.9), channel_id=1, source_target_pairs={{3,2},{0,3},{5,4},{6,5},{7,6},{4,7},{1,0},{2,1},{11,10},{8,11},{13... | collective-permute-start | bytes 3145736 | tf_op jit(solution)/shard_map/ppermute | solution.py:248
  56.9 2.4 %first_step.9 = (f32[2,1,256,256]{3,2,1,0:T(8,128)S(1)}, f32[2,256,256]{2,1,0:T(8,128)S(1)}, f32[8,128]{1,0:T(8,128)S(1)}) custom-call(f32[2,8,256,256]{3,2,1,0:T(8,128)S(1)} %bitcast.65, f32[2,256,256]{2,1,0:T(8,128)S(1)} %collective-permute-done.3.a_ref, f32[2,256,256]{2,1,0:T(8,128)S(1)} %pad_maximum_fusion.1.q_ref, ...), custom_call_target="tpu_custom_call", output_to_operand_aliasing={{1}: (4, {}), {2}: (5, {})} | custom-call | flops 3000000000 | bytes 400000 | tf_op jit(solution)/shard_map/first_step/pallas_call | solution.py:176
  59.2 0.3 collective-permute-start.11
  59.5 2.4 %first_step.10 = (f32[2,1,256,256]{3,2,1,0:T(8,128)S(1)}, f32[2,256,256]{2,1,0:T(8,128)S(1)}, f32[8,128]{1,0:T(8,128)S(1)}) custom-call(f32[2,2,256,256]{3,2,1,0:T(8,128)S(1)} %collective-permute-done.1.f_ref, f32[8,256,256]{2,1,0:T(8,128)S(1)} %bitcast.52, f32[2,256,256]{2,1,0:T(8,128)S(1)} %pad_maximum_fusion.q_ref, ...), custom_call_target="tpu_custom_call", output_to_operand_aliasing={{1}: (4, {}), {2}: (5, {})} | custom-call | flops 100000000 | bytes 400000 | tf_op jit(solution)/shard_map/first_step/pallas_call | solution.py:176
  61.9 0.4 collective-permute-start.8
  62.3 2.3 %collective-permute-done.6 = f32[2,1,256,256]{3,2,1,0:T(8,128)S(1)} collective-permute-done((f32[2,1,256,256]{3,2,1,0:T(8,128)S(1)}, f32[2,1,256,256]{3,2,1,0:T(8,128)S(1)}, u32[]{:S(2)}, u32[]{:S(2)}) %collective-permute-start.6) | collective-permute-done | bytes 524320 | tf_op jit(solution)/shard_map/ppermute | solution.py:248
  64.7 3.4 %collective-permute-start.7 = (f32[2,1,256,256]{3,2,1,0:T(8,128)S(1)}, f32[2,1,256,256]{3,2,1,0:T(8,128)S(1)}, u32[]{:S(2)}, u32[]{:S(2)}) collective-permute-start(f32[2,1,256,256]{3,2,1,0:T(8,128)S(1)} %collective-permute-done.6), channel_id=1, source_target_pairs={{3,2},{0,3},{5,4},{6,5},{7,6},{4,7},{1,0},{2,1},{11,10},{8,11},{13... | collective-permute-start | bytes 1572872 | tf_op jit(solution)/shard_map/ppermute | solution.py:248
  68.1 2.4 %first_step.11 = (f32[2,1,256,256]{3,2,1,0:T(8,128)S(1)}, f32[2,256,256]{2,1,0:T(8,128)S(1)}, f32[8,128]{1,0:T(8,128)S(1)}) custom-call(f32[2,2,256,256]{3,2,1,0:T(8,128)S(1)} %collective-permute-done.1.f_ref, f32[8,256,256]{2,1,0:T(8,128)S(1)} %bitcast.53, f32[2,256,256]{2,1,0:T(8,128)S(1)} %pad_maximum_fusion.q_ref, ...), custom_call_target="tpu_custom_call", output_to_operand_aliasing={{1}: (4, {}), {2}: (5, {})} | custom-call | flops 5000000000 | bytes 400000 | tf_op jit(solution)/shard_map/first_step/pallas_call | solution.py:176
  70.5 4.5 %collective-permute-done.12.s_ref = f32[2,2,256,256]{3,2,1,0:T(8,128)S(1)} collective-permute-done((f32[2,2,256,256]{3,2,1,0:T(8,128)S(1)}, f32[2,2,256,256]{3,2,1,0:T(8,128)S(1)}, u32[]{:S(2)}, u32[]{:S(2)}) %collective-permute-start.12) | collective-permute-done | bytes 1048608 | tf_op jit(solution)/shard_map/ppermute | solution.py:248
  75.0 4.2 %second_step.6 = (f32[2,8,256,256]{3,2,1,0:T(8,128)}, f32[2,256,256]{2,1,0:T(8,128)S(1)}, f32[8,128]{1,0:T(8,128)S(1)}) custom-call(f32[2,2,256,256]{3,2,1,0:T(8,128)S(1)} %collective-permute-done.12.s_ref, f32[8,256,256]{2,1,0:T(8,128)S(1)} %bitcast.54, f32[2,256,256]{2,1,0:T(8,128)S(1)} %pad_maximum_fusion.q_ref, ...), custom_call_target="tpu_custom_call", output_to_operand_aliasing={{1}: (4, {}), {2}: (5, {})} | custom-call | flops 100000000 | bytes 800000 | tf_op jit(solution)/shard_map/second_step/pallas_call | solution.py:176
  79.2 7.9 %collective-permute-done.11.s_ref = f32[2,1,256,256]{3,2,1,0:T(8,128)S(1)} collective-permute-done((f32[2,1,256,256]{3,2,1,0:T(8,128)S(1)}, f32[2,1,256,256]{3,2,1,0:T(8,128)S(1)}, u32[]{:S(2)}, u32[]{:S(2)}) %collective-permute-start.11) | collective-permute-done | bytes 524320 | tf_op jit(solution)/shard_map/ppermute | solution.py:248
  87.1 2.4 %second_step.7 = (f32[2,8,256,256]{3,2,1,0:T(8,128)}, f32[2,256,256]{2,1,0:T(8,128)S(1)}, f32[8,128]{1,0:T(8,128)S(1)}) custom-call(f32[2,1,256,256]{3,2,1,0:T(8,128)S(1)} %collective-permute-done.11.s_ref, f32[8,256,256]{2,1,0:T(8,128)S(1)} %bitcast.55, ...), custom_call_target="tpu_custom_call", output_to_operand_aliasing={{1}: (4, {}), {2}: (5, {}), {0}: (6, {})} | custom-call | flops 100000000 | bytes 400000 | tf_op jit(solution)/shard_map/second_step/pallas_call | solution.py:176
  89.5 4.2 %second_step.8 = (f32[2,8,256,256]{3,2,1,0:T(8,128)}, f32[2,256,256]{2,1,0:T(8,128)S(1)}, f32[8,128]{1,0:T(8,128)S(1)}) custom-call(f32[2,2,256,256]{3,2,1,0:T(8,128)S(1)} %collective-permute-done.10.s_ref, f32[8,256,256]{2,1,0:T(8,128)S(1)} %bitcast.56, ...), custom_call_target="tpu_custom_call", output_to_operand_aliasing={{1}: (4, {}), {2}: (5, {}), {0}: (6, {})} | custom-call | flops 100000000 | bytes 800000 | tf_op jit(solution)/shard_map/second_step/pallas_call | solution.py:176
  93.7 3.8 %collective-permute-done.8.s_ref = f32[2,1,256,256]{3,2,1,0:T(8,128)S(1)} collective-permute-done((f32[2,1,256,256]{3,2,1,0:T(8,128)S(1)}, f32[2,1,256,256]{3,2,1,0:T(8,128)S(1)}, u32[]{:S(2)}, u32[]{:S(2)}) %collective-permute-start.8) | collective-permute-done | bytes 524320 | tf_op jit(solution)/shard_map/ppermute | solution.py:248
  97.5 2.4 %second_step.9 = (f32[2,8,256,256]{3,2,1,0:T(8,128)}, f32[2,256,256]{2,1,0:T(8,128)S(1)}, f32[8,128]{1,0:T(8,128)S(1)}) custom-call(f32[2,1,256,256]{3,2,1,0:T(8,128)S(1)} %collective-permute-done.8.s_ref, f32[8,256,256]{2,1,0:T(8,128)S(1)} %bitcast.57, ...), custom_call_target="tpu_custom_call", output_to_operand_aliasing={{1}: (4, {}), {2}: (5, {}), {0}: (6, {})} | custom-call | flops 1000000000 | bytes 400000 | tf_op jit(solution)/shard_map/second_step/pallas_call | solution.py:176
  99.9 9.7 %collective-permute-done.7.s_ref = f32[2,1,256,256]{3,2,1,0:T(8,128)S(1)} collective-permute-done((f32[2,1,256,256]{3,2,1,0:T(8,128)S(1)}, f32[2,1,256,256]{3,2,1,0:T(8,128)S(1)}, u32[]{:S(2)}, u32[]{:S(2)}) %collective-permute-start.7) | collective-permute-done | bytes 524320 | tf_op jit(solution)/shard_map/ppermute | solution.py:248
  109.6 2.4 %second_step.10 = (f32[2,8,256,256]{3,2,1,0:T(8,128)}, f32[2,256,256]{2,1,0:T(8,128)S(1)}, f32[8,128]{1,0:T(8,128)S(1)}) custom-call(f32[2,1,256,256]{3,2,1,0:T(8,128)S(1)} %collective-permute-done.7.s_ref, f32[8,256,256]{2,1,0:T(8,128)S(1)} %bitcast.58, ...), custom_call_target="tpu_custom_call", output_to_operand_aliasing={{1}: (4, {}), {2}: (5, {}), {0}: (6, {})} | custom-call | flops 1000000000 | bytes 400000 | tf_op jit(solution)/shard_map/second_step/pallas_call | solution.py:176
  112.0 2.4 %second_step.11 = (f32[2,8,256,256]{3,2,1,0:T(8,128)}, f32[2,256,256]{2,1,0:T(8,128)S(1)}, f32[8,128]{1,0:T(8,128)S(1)}) custom-call(f32[2,1,256,256]{3,2,1,0:T(8,128)S(1)} %collective-permute-done.5.s_ref, f32[8,256,256]{2,1,0:T(8,128)S(1)} %bitcast.59, ...), custom_call_target="tpu_custom_call", output_to_operand_aliasing={{1}: (4, {}), {2}: (5, {}), {0}: (6, {})} | custom-call | flops 1000000000 | bytes 400000 | tf_op jit(solution)/shard_map/second_step/pallas_call | solution.py:176
  114.5 0.9 finish.1
  115.4 25.7 %all_to_all.11 = f32[128,8,128]{2,1,0:T(8,128)S(1)} all-to-all(f32[128,8,128]{2,1,0:T(8,128)S(1)} %bitcast.60), channel_id=1, replica_groups=mesh['tile'=16,'plane'=8] {'tile','plane'}, dimensions={0} | all-to-all | bytes 1048576 | tf_op jit(solution)/shard_map/all_to_all | solution.py:228
  141.1 0.1 reduce_sum.9
  141.3 17.8 %all_to_all.10 = f32[128,8,128]{2,1,0:T(8,128)S(1)} all-to-all(f32[128,8,128]{2,1,0:T(8,128)S(1)} %broadcast_in_dim.14), channel_id=1, replica_groups=mesh['tile'=16,'plane'=8] {'tile','plane'}, dimensions={0} | all-to-all | bytes 1048576 | tf_op jit(solution)/shard_map/all_to_all | solution.py:230
  159.1 0.2 copy.43
  159.3 1.0 copy.45
  (23 shorter events, 0.3 us)
Async XLA Ops:
  0.6 8.7 %copy-start = (f32[2,256,256]{2,1,0:T(8,128)S(1)}, f32[2,256,256]{2,1,0:T(8,128)}, u32[]{:S(2)}) copy-start(f32[2,256,256]{2,1,0:T(8,128)} %param.12) | copy-start | bytes 1572868
  0.6 10.3 %copy-start.5 = (f32[256,256,1]{1,0,2:T(8,128)S(1)}, f32[256,256,1]{1,0,2:T(8,128)}, u32[]{:S(2)}) copy-start(f32[256,256,1]{1,0,2:T(8,128)} %constant.21) | copy-start | bytes 786436
  0.7 11.6 %copy-start.6 = (f32[256,256]{1,0:T(8,128)S(1)}, f32[256,256]{1,0:T(8,128)}, u32[]{:S(2)}) copy-start(f32[256,256]{1,0:T(8,128)} %constant.16.clone) | copy-start | bytes 786436
  0.7 11.6 %collective-permute-start = (f32[1]{0:T(128)}, f32[1]{0:T(128)}, u32[]{:S(2)}, u32[]{:S(2)}) collective-permute-start(f32[1]{0:T(128)} %param.13), channel_id=1, source_target_pairs={{0,1},{1,2},{2,3},{3,4},{4,5},{5,6},{6,7},{7,0},{8,9},{9,10},{10,1... | collective-permute-start | bytes 20 | tf_op jit(solution)/shard_map/ppermute | solution.py:248
  4.2 10.8 %copy-start.3 = (f32[2,1,8,256,256]{4,3,2,1,0:T(8,128)S(1)}, f32[2,1,8,256,256]{4,3,2,1,0:T(8,128)}, u32[]{:S(2)}) copy-start(f32[2,1,8,256,256]{4,3,2,1,0:T(8,128)} %param.10) | copy-start | bytes 12582916
  4.2 29.2 %collective-permute-start.2 = (f32[2,2,256,256]{3,2,1,0:T(8,128)S(1)}, f32[2,2,256,256]{3,2,1,0:T(8,128)S(1)}, u32[]{:S(2)}, u32[]{:S(2)}) collective-permute-start(f32[2,2,256,256]{3,2,1,0:T(8,128)S(1)} %slice.32), channel_id=1, source_target_pairs={{0,1},{1,2},{2,3},{3,4},{4,5},{5,6},{6,7},{7,0},{8,9},{9,10},{10,1... | collective-permute-start | bytes 3145736 | tf_op jit(solution)/shard_map/ppermute | solution.py:248
  6.6 8.5 %copy-start.1 = (f32[1,8,256,256]{3,2,1,0:T(8,128)S(1)}, f32[1,8,256,256]{3,2,1,0:T(8,128)}, u32[]{:S(2)}) copy-start(f32[1,8,256,256]{3,2,1,0:T(8,128)} %param.11) | copy-start | bytes 6291460
  6.6 13.1 %collective-permute-start.4 = (f32[2,256,256]{2,1,0:T(8,128)S(1)}, f32[2,256,256]{2,1,0:T(8,128)S(1)}, u32[]{:S(2)}, u32[]{:S(2)}) collective-permute-start(f32[2,256,256]{2,1,0:T(8,128)S(1)} %slice_bitcast_fusion), channel_id=1, source_target_pairs={{0,7},{1,0},{2,1},{3,2},{4,3},{5,4},{6,5},{7,6},{8,15},{9,8},{10,9... | collective-permute-start | bytes 1572872 | tf_op jit(solution)/shard_map/ppermute | solution.py:248
  12.2 7.6 %copy-start.2 = (bf16[2,4,256,256]{3,2,1,0:T(8,128)(2,1)S(1)}, bf16[2,4,256,256]{3,2,1,0:T(8,128)(2,1)}, u32[]{:S(2)}) copy-start(bf16[2,4,256,256]{3,2,1,0:T(8,128)(2,1)} %constant.4.clone.tables) | copy-start | bytes 3145732
  15.1 44.5 %collective-permute-start.1 = (f32[2,2,256,256]{3,2,1,0:T(8,128)S(1)}, f32[2,2,256,256]{3,2,1,0:T(8,128)S(1)}, u32[]{:S(2)}, u32[]{:S(2)}) collective-permute-start(f32[2,2,256,256]{3,2,1,0:T(8,128)S(1)} %slice.25), channel_id=1, source_target_pairs={{0,1},{1,2},{2,3},{3,4},{4,5},{5,6},{6,7},{7,0},{8,9},{9,10},{10,1... | collective-permute-start | bytes 3145736 | tf_op jit(solution)/shard_map/ppermute | solution.py:248
  15.2 15.8 %collective-permute-start.3 = (f32[2,256,256]{2,1,0:T(8,128)S(1)}, f32[2,256,256]{2,1,0:T(8,128)S(1)}, u32[]{:S(2)}, u32[]{:S(2)}) collective-permute-start(f32[2,256,256]{2,1,0:T(8,128)S(1)} %slice.27), channel_id=1, source_target_pairs={{0,7},{1,0},{2,1},{3,2},{4,3},{5,4},{6,5},{7,6},{8,15},{9,8},{10,9... | collective-permute-start | bytes 1572872 | tf_op jit(solution)/shard_map/ppermute | solution.py:248
  24.8 28.6 %collective-permute-start.9 = (f32[2,2,256,256]{3,2,1,0:T(8,128)S(1)}, f32[2,2,256,256]{3,2,1,0:T(8,128)S(1)}, u32[]{:S(2)}, u32[]{:S(2)}) collective-permute-start(f32[2,2,256,256]{3,2,1,0:T(8,128)S(1)} %get-tuple-element.55), channel_id=1, source_target_pairs={{0,3},{1,0},{2,5},{3,6},{4,7},{5,4},{6,1},{7,2},{8,11},{9,8},{10,1... | collective-permute-start | bytes 3145736 | tf_op jit(solution)/shard_map/ppermute | solution.py:248
  38.4 36.6 %collective-permute-start.12 = (f32[2,2,256,256]{3,2,1,0:T(8,128)S(1)}, f32[2,2,256,256]{3,2,1,0:T(8,128)S(1)}, u32[]{:S(2)}, u32[]{:S(2)}) collective-permute-start(f32[2,2,256,256]{3,2,1,0:T(8,128)S(1)} %get-tuple-element.57), channel_id=1, source_target_pairs={{0,1},{1,2},{2,3},{3,4},{4,5},{5,6},{6,7},{7,0},{8,9},{9,10},{10,1... | collective-permute-start | bytes 3145736 | tf_op jit(solution)/shard_map/ppermute | solution.py:248
  39.0 25.7 %collective-permute-start.6 = (f32[2,1,256,256]{3,2,1,0:T(8,128)S(1)}, f32[2,1,256,256]{3,2,1,0:T(8,128)S(1)}, u32[]{:S(2)}, u32[]{:S(2)}) collective-permute-start(f32[2,1,256,256]{3,2,1,0:T(8,128)S(1)} %get-tuple-element.53), channel_id=1, source_target_pairs={{0,3},{1,0},{2,5},{3,6},{4,7},{5,4},{6,1},{7,2},{8,11},{9,8},{10,1... | collective-permute-start | bytes 1572872 | tf_op jit(solution)/shard_map/ppermute | solution.py:248
  53.5 36.1 %collective-permute-start.10 = (f32[2,2,256,256]{3,2,1,0:T(8,128)S(1)}, f32[2,2,256,256]{3,2,1,0:T(8,128)S(1)}, u32[]{:S(2)}, u32[]{:S(2)}) collective-permute-start(f32[2,2,256,256]{3,2,1,0:T(8,128)S(1)} %collective-permute-done.9), channel_id=1, source_target_pairs={{3,2},{0,3},{5,4},{6,5},{7,6},{4,7},{1,0},{2,1},{11,10},{8,11},{13... | collective-permute-start | bytes 3145736 | tf_op jit(solution)/shard_map/ppermute | solution.py:248
  59.2 27.9 %collective-permute-start.11 = (f32[2,1,256,256]{3,2,1,0:T(8,128)S(1)}, f32[2,1,256,256]{3,2,1,0:T(8,128)S(1)}, u32[]{:S(2)}, u32[]{:S(2)}) collective-permute-start(f32[2,1,256,256]{3,2,1,0:T(8,128)S(1)} %get-tuple-element.56), channel_id=1, source_target_pairs={{0,2},{1,3},{2,4},{3,5},{4,6},{5,7},{6,0},{7,1},{8,10},{9,11},{10,... | collective-permute-start | bytes 1572872 | tf_op jit(solution)/shard_map/ppermute | solution.py:248
  61.9 35.6 %collective-permute-start.8 = (f32[2,1,256,256]{3,2,1,0:T(8,128)S(1)}, f32[2,1,256,256]{3,2,1,0:T(8,128)S(1)}, u32[]{:S(2)}, u32[]{:S(2)}) collective-permute-start(f32[2,1,256,256]{3,2,1,0:T(8,128)S(1)} %get-tuple-element.54), channel_id=1, source_target_pairs={{0,1},{1,2},{2,3},{3,4},{4,5},{5,6},{6,7},{7,0},{8,9},{9,10},{10,1... | collective-permute-start | bytes 1572872 | tf_op jit(solution)/shard_map/ppermute | solution.py:248
  64.7 44.9 %collective-permute-start.7 = (f32[2,1,256,256]{3,2,1,0:T(8,128)S(1)}, f32[2,1,256,256]{3,2,1,0:T(8,128)S(1)}, u32[]{:S(2)}, u32[]{:S(2)}) collective-permute-start(f32[2,1,256,256]{3,2,1,0:T(8,128)S(1)} %collective-permute-done.6), channel_id=1, source_target_pairs={{3,2},{0,3},{5,4},{6,5},{7,6},{4,7},{1,0},{2,1},{11,10},{8,11},{13... | collective-permute-start | bytes 1572872 | tf_op jit(solution)/shard_map/ppermute | solution.py:248
  75.0 37.0 %collective-permute-start.5 = (f32[2,1,256,256]{3,2,1,0:T(8,128)S(1)}, f32[2,1,256,256]{3,2,1,0:T(8,128)S(1)}, u32[]{:S(2)}, u32[]{:S(2)}) collective-permute-start(f32[2,1,256,256]{3,2,1,0:T(8,128)S(1)} %get-tuple-element.52), channel_id=1, source_target_pairs={{0,1},{1,2},{2,3},{3,4},{4,5},{5,6},{6,7},{7,0},{8,9},{9,10},{10,1... | collective-permute-start | bytes 1572872 | tf_op jit(solution)/shard_map/ppermute | solution.py:248
  112.0 2.4 %copy-start.4 = (bf16[2,256,256]{2,1,0:T(8,128)(2,1)S(1)}, bf16[2,256,256]{2,1,0:T(8,128)(2,1)}, u32[]{:S(2)}) copy-start(bf16[2,256,256]{2,1,0:T(8,128)(2,1)} %constant.17.clone.mix) | copy-start | bytes 786436
where the time goes:
time: 161 us; the launch traced here: 160 us
  blocking collectives  43.5 us (27%)
  waiting for transfers between devices  42.2 us (26%)
  Pallas kernels  38.4 us (24%)
  starting transfers between devices  25.8 us (16%)
  local copies, waits for them, and re-layouts  3.84 us (2%)
  other arithmetic  2.89 us (2%)
  matrix products  2.18 us (1%)
    ppermute x13, waiting for transfers between devices, sent(): return lax.ppermute(value, 'plane', pairs)  42.2 us
    pallas_call x12, Pallas kernels, step_call(): pl.pallas_call(kernel, grid=(tiles,), in_specs=[tile_spec(x.shape, x_at),...  37.4 us
    ppermute x13, starting transfers between devices, sent(): return lax.ppermute(value, 'plane', pairs)  25.8 us
    all_to_all x1, blocking collectives, summed(): mine = lax.all_to_all(mine, AXES, 0, 0, tiled=True).sum(0)  25.7 us
    all_to_all x1, blocking collectives, summed(): lax.all_to_all(mine, AXES, 0, 0, tiled=True).reshape(2, 2, WIDTH, HALF)  17.8 us
  transfers between devices with their start and end apart: 13, of which 8 were waited for; matrix products, arithmetic and copies ran while one was open for 5% of the time, Pallas kernels for 22%

commit v1 on v0

--- a/solution.py
+++ b/solution.py
@@ -191,15 +191,18 @@
     )(x, amps, q, tables, grad, *more)
 
 
-def finish_kernel(a_ref, b_ref, ta_re, ta_im, tb_re, tb_im, mix, factor_ref, out_ref):
+def finish_kernel(a_ref, b_ref, ta_re, ta_im, tb_re, tb_im, mix, factor_ref, core_ref, mine_ref, others_ref):
     a = product_conj(a_ref[0], a_ref[1], ta_re[...], ta_im[...])
     b = product_conj(b_ref[0], b_ref[1], tb_re[...], tb_im[...])
+    parts = []
     for part in (0, 1):
         x = (a[part] + b[part]) * factor_ref[0]
         x = sum(dot(mix[1], piece) for piece in pieces(x))
-        x = sum(dot(piece, mix[0]) for piece in pieces(x))
-        out_ref[part, 0] = x[:, :HALF]
-        out_ref[part, 1] = x[:, HALF:]
+        parts.append(sum(dot(piece, mix[0]) for piece in pieces(x)))
+    first_core = core_ref[0] == 0
+    for ref, x in ((mine_ref, jnp.where(first_core, *parts)), (others_ref, jnp.where(first_core, *parts[::-1]))):
+        ref[0] = x[:, :HALF]
+        ref[1] = x[:, HALF:]
 
 
 def pieces(x):
@@ -209,25 +212,31 @@
     return high, middle, (x - middle.astype(F32)).astype(BF16)
 
 
-def finished(grad_a, grad_b, turn_a, turn_b, mix, factor):
-    vmem = pl.BlockSpec(memory_space=pltpu.VMEM)
+def finished(grad_a, grad_b, turn_a, turn_b, mix, factor, core):
+    vmem, smem = pl.BlockSpec(memory_space=pltpu.VMEM), pl.BlockSpec(memory_space=pltpu.SMEM)
     both = jnp.asarray(np.stack([mix, mix.T]).astype(BF16))
+    part = jax.ShapeDtypeStruct((2, WIDTH, HALF), F32)
     return pl.pallas_call(
         finish_kernel,
-        in_specs=[vmem] * 7 + [pl.BlockSpec(memory_space=pltpu.SMEM)],
-        out_specs=vmem,
-        out_shape=jax.ShapeDtypeStruct((2, 2, WIDTH, HALF), F32),
+        in_specs=[vmem] * 7 + [smem] * 2,
+        out_specs=[vmem] * 2,
+        out_shape=[part] * 2,
         compiler_params=pltpu.CompilerParams(vmem_limit_bytes=40 * 1024 * 1024),
         name="finish",
-    )(grad_a, grad_b, *turn_a, *turn_b, both, jnp.full((1,), factor, F32))
-
-
-def summed(parts):
-    members = lax.axis_size("tile") * lax.axis_size("plane")
-    mine = parts.reshape(members, -1, HALF)
-    mine = lax.all_to_all(mine, AXES, 0, 0, tiled=True).sum(0)
+    )(grad_a, grad_b, *turn_a, *turn_b, both, jnp.full((1,), factor, F32), jnp.full((1,), core, jnp.int32))
+
+
+def summed(mine, others, core):
+    tiles, planes = lax.axis_size("tile"), lax.axis_size("plane")
+    groups = [[t * planes + p for t in range(c, tiles, 2) for p in range(planes)] for c in (0, 1)]
+    members = len(groups[0])
+    swap = [(t * planes + p, (t ^ 1) * planes + p) for t in range(tiles) for p in range(planes)]
+    mine = (mine + lax.ppermute(others, AXES, swap)).reshape(members, -1, HALF)
+    mine = lax.all_to_all(mine, AXES, 0, 0, tiled=True, axis_index_groups=groups).sum(0)
     mine = jnp.broadcast_to(mine[None], (members, *mine.shape))
-    total = lax.all_to_all(mine, AXES, 0, 0, tiled=True).reshape(2, 2, WIDTH, HALF)
+    mine = lax.all_to_all(mine, AXES, 0, 0, tiled=True, axis_index_groups=groups).reshape(2, WIDTH, HALF)
+    others = lax.ppermute(mine, AXES, swap)
+    total = jnp.where(core == 0, jnp.stack([mine, others]), jnp.stack([others, mine]))
     return total.transpose(0, 2, 1, 3).reshape(2, WIDTH, WIDTH)
 
 
@@ -294,8 +303,9 @@
     second(s_6, 6, 1, weights[7])
     second(s_3, 3, 1, weights[7])
 
-    parts = finished(grads["before"], grads["here"], turn_before, turn_here, mix, 2.0 * factor)
-    return (out[:, None], summed(parts))
+    core = lax.axis_index("tile") % 2
+    mine, others = finished(grads["before"], grads["here"], turn_before, turn_here, mix, 2.0 * factor, core)
+    return (out[:, None], summed(mine, others, core))
 
 
 def solution(mesh):

time: 161 us -> 163 us (1.012)
  blocking collectives: 43.5 us -> 35.9 us
  waiting for transfers between devices: 42.2 us -> 34.7 us
  Pallas kernels: 38.4 us -> 45.6 us
  starting transfers between devices: 25.8 us -> 30.5 us
  local copies, waits for them, and re-layouts: 3.84 us -> 8.32 us
    ppermute x13, waiting for transfers between devices: 42.2 us -> 32.3 us  [sent(): return lax.ppermute(value, 'plane', pairs)]
    all_to_all x2, blocking collectives: 43.5 us -> 35.9 us  [summed(): lax.all_to_all(mine, AXES, 0, 0, tiled=True, axis_index_groups=groups)]
    pallas_call x12, Pallas kernels: 37.4 us -> 44.6 us  [step_call(): pl.pallas_call(kernel, grid=(tiles,), in_specs=[tile_spec(x.shape, x_at),...]
    ppermute x0 -> x2, starting transfers between devices: none -> 4.63 us  [the longest x1 3.17 us: summed(): others = lax.ppermute(mine, AXES, swap)]
    unnamed x15 -> x35, local copies, waits for them, and re-layouts: 1.04 us -> 5.53 us
    ppermute x0 -> x2, waiting for transfers between devices: none -> 2.32 us  [the longest x1 1.16 us: summed(): others = lax.ppermute(mine, AXES, swap)]
  transfers between devices with their start and end apart: 13 -> 15, of which waited for: 8 -> 9; matrix products, arithmetic and copies ran while one was open for 5% -> 5% of each run, Pallas kernels for 22% -> 25%
where the time goes in v1:
time: 163 us; the launch traced here: 162 us
  Pallas kernels  45.6 us (28%)
  blocking collectives  35.9 us (22%)
  waiting for transfers between devices  34.7 us (21%)
  starting transfers between devices  30.5 us (19%)
  local copies, waits for them, and re-layouts  8.32 us (5%)
  other arithmetic  3.71 us (2%)
  matrix products  2.18 us (1%)
    pallas_call x12, Pallas kernels, step_call(): pl.pallas_call(kernel, grid=(tiles,), in_specs=[tile_spec(x.shape, x_at),...  44.6 us
    all_to_all x2, blocking collectives, summed(): lax.all_to_all(mine, AXES, 0, 0, tiled=True, axis_index_groups=groups)  35.9 us
    ppermute x13, waiting for transfers between devices, sent(): return lax.ppermute(value, 'plane', pairs)  32.3 us
    ppermute x13, starting transfers between devices, sent(): return lax.ppermute(value, 'plane', pairs)  25.8 us
    unnamed x35, local copies, waits for them, and re-layouts  5.53 us
    another operation x2, other arithmetic, body(): q_here = jnp.stack(product(shuffled[0], shuffled[1], *turn_here))  3.54 us
  transfers between devices with their start and end apart: 15, of which 9 were waited for; matrix products, arithmetic and copies ran while one was open for 5% of the time, Pallas kernels for 25%

profile of v1, /device:TPU:1, one launch (start us, length us, event | category | flops | bytes accessed | tf_op | source)
XLA Modules:
  0.0 162.4 jit_solution(3674822341346978279)
XLA Ops:
  0.7 2.2 %collective-permute-start = (f32[1]{0:T(128)}, f32[1]{0:T(128)}, u32[]{:S(2)}, u32[]{:S(2)}) collective-permute-start(f32[1]{0:T(128)} %param.13), channel_id=1, source_target_pairs={{0,1},{1,2},{2,3},{3,4},{4,5},{5,6},{6,7},{7,0},{8,9},{9,10},{10,1... | collective-permute-start | bytes 20 | tf_op jit(solution)/shard_map/ppermute | solution.py:257
  2.9 1.3 slice.32
  4.2 1.4 collective-permute-start.2
  5.6 1.1 slice_bitcast_fusion
  6.6 2.7 %collective-permute-start.4 = (f32[2,256,256]{2,1,0:T(8,128)S(1)}, f32[2,256,256]{2,1,0:T(8,128)S(1)}, u32[]{:S(2)}, u32[]{:S(2)}) collective-permute-start(f32[2,256,256]{2,1,0:T(8,128)S(1)} %slice_bitcast_fusion), channel_id=1, source_target_pairs={{0,7},{1,0},{2,1},{3,2},{4,3},{5,4},{6,5},{7,6},{8,15},{9,8},{10,9... | collective-permute-start | bytes 1572872 | tf_op jit(solution)/shard_map/ppermute | solution.py:257
  9.4 1.6 convolution_bitcast_fusion
  11.0 0.6 fusion.1
  12.3 3.5 %subtract_bitcast_fusion = (f32[1,256,256]{2,1,0:T(8,128)S(1)}, f32[1,256,256]{2,1,0:T(8,128)S(1)}, f32[1,256,256]{2,1,0:T(8,128)S(1)}, f32[1,256,256]{2,1,0:T(8...) fusion(f32[2,256,256]{2,1,0:T(8,128)S(1)} %fusion.1, ...), kind=kLoop, calls=%fused_computation.13 | loop fusion | flops 917504 | bytes 2883592 | tf_op jit(solution)/shard_map/stack | solution.py:268
  15.8 0.1 slice.25
  16.1 3.6 %collective-permute-start.3 = (f32[2,256,256]{2,1,0:T(8,128)S(1)}, f32[2,256,256]{2,1,0:T(8,128)S(1)}, u32[]{:S(2)}, u32[]{:S(2)}) collective-permute-start(f32[2,256,256]{2,1,0:T(8,128)S(1)} %slice.27), channel_id=1, source_target_pairs={{0,7},{1,0},{2,1},{3,2},{4,3},{5,4},{6,5},{7,6},{8,15},{9,8},{10,9... | collective-permute-start | bytes 1572872 | tf_op jit(solution)/shard_map/ppermute | solution.py:257
  19.8 5.0 %first_step.6 = (f32[2,2,256,256]{3,2,1,0:T(8,128)S(1)}, f32[2,256,256]{2,1,0:T(8,128)S(1)}, f32[8,128]{1,0:T(8,128)S(1)}) custom-call(f32[2,8,256,256]{3,2,1,0:T(8,128)S(1)} %bitcast.65, f32[2,256,256]{2,1,0:T(8,128)S(1)} %collective-permute-done.4.a_ref, f32[2,256,256]{2,1,0:T(8,128)S(1)} %pad_maximum_fusion.1.q_ref, ...), custom_call_target="tpu_custom_call", output_to_operand_aliasing={{1}: (4, {}), {2}: (5, {})} | custom-call | flops 30000001024 | bytes 800000 | tf_op jit(solution)/shard_map/first_step/pallas_call | solution.py:176
  24.8 4.1 %collective-permute-start.9 = (f32[2,2,256,256]{3,2,1,0:T(8,128)S(1)}, f32[2,2,256,256]{3,2,1,0:T(8,128)}, u32[]{:S(2)}, u32[]{:S(2)}) collective-permute-start(f32[2,2,256,256]{3,2,1,0:T(8,128)S(1)} %get-tuple-element.57), channel_id=1, source_target_pairs={{0,3},{1,0},{2,5},{3,6},{4,7},{5,4},{6,1},{7,2},{8,11},{9,8},{10,1... | collective-permute-start | bytes 3145736 | tf_op jit(solution)/shard_map/ppermute | solution.py:257
  28.9 2.5 %collective-permute-done.3.a_ref = f32[2,256,256]{2,1,0:T(8,128)S(1)} collective-permute-done((f32[2,256,256]{2,1,0:T(8,128)S(1)}, f32[2,256,256]{2,1,0:T(8,128)S(1)}, u32[]{:S(2)}, u32[]{:S(2)}) %collective-permute-start.3) | collective-permute-done | bytes 524320 | tf_op jit(solution)/shard_map/ppermute | solution.py:257
  31.4 2.3 %first_step.7 = (f32[2,1,256,256]{3,2,1,0:T(8,128)S(1)}, f32[2,256,256]{2,1,0:T(8,128)S(1)}, f32[8,128]{1,0:T(8,128)S(1)}) custom-call(f32[2,8,256,256]{3,2,1,0:T(8,128)S(1)} %bitcast.66, f32[2,256,256]{2,1,0:T(8,128)S(1)} %collective-permute-done.3.a_ref, f32[2,256,256]{2,1,0:T(8,128)S(1)} %pad_maximum_fusion.1.q_ref, ...), custom_call_target="tpu_custom_call", output_to_operand_aliasing={{1}: (4, {}), {2}: (5, {})} | custom-call | flops 3000000000 | bytes 400000 | tf_op jit(solution)/shard_map/first_step/pallas_call | solution.py:176
  33.8 5.0 %first_step.8 = (f32[2,2,256,256]{3,2,1,0:T(8,128)S(1)}, f32[2,256,256]{2,1,0:T(8,128)S(1)}, f32[8,128]{1,0:T(8,128)S(1)}) custom-call(f32[2,2,256,256]{3,2,1,0:T(8,128)S(1)} %collective-permute-done.2.f_ref, f32[8,256,256]{2,1,0:T(8,128)S(1)} %bitcast.54, f32[2,256,256]{2,1,0:T(8,128)S(1)} %pad_maximum_fusion.q_ref, ...), custom_call_target="tpu_custom_call", output_to_operand_aliasing={{1}: (4, {}), {2}: (5, {})} | custom-call | flops 30000001024 | bytes 800000 | tf_op jit(solution)/shard_map/first_step/pallas_call | solution.py:176
  38.7 0.2 collective-permute-start.12
  39.0 4.0 %collective-permute-start.6 = (f32[2,1,256,256]{3,2,1,0:T(8,128)S(1)}, f32[2,1,256,256]{3,2,1,0:T(8,128)}, u32[]{:S(2)}, u32[]{:S(2)}) collective-permute-start(f32[2,1,256,256]{3,2,1,0:T(8,128)S(1)} %get-tuple-element.55), channel_id=1, source_target_pairs={{0,3},{1,0},{2,5},{3,6},{4,7},{5,4},{6,1},{7,2},{8,11},{9,8},{10,1... | collective-permute-start | bytes 1572872 | tf_op jit(solution)/shard_map/ppermute | solution.py:257
  42.9 10.9 %collective-permute-done.9 = f32[2,2,256,256]{3,2,1,0:T(8,128)} collective-permute-done((f32[2,2,256,256]{3,2,1,0:T(8,128)S(1)}, f32[2,2,256,256]{3,2,1,0:T(8,128)}, u32[]{:S(2)}, u32[]{:S(2)}) %collective-permute-start.9) | collective-permute-done | bytes 1048608 | tf_op jit(solution)/shard_map/ppermute | solution.py:257
  53.8 3.5 %collective-permute-start.10 = (f32[2,2,256,256]{3,2,1,0:T(8,128)}, f32[2,2,256,256]{3,2,1,0:T(8,128)}, u32[]{:S(2)}, u32[]{:S(2)}) collective-permute-start(f32[2,2,256,256]{3,2,1,0:T(8,128)} %collective-permute-done.9), channel_id=1, source_target_pairs={{3,2},{0,3},{5,4},{6,5},{7,6},{4,7},{1,0},{2,1},{11,10},{8,11},{13... | collective-permute-start | bytes 3145736 | tf_op jit(solution)/shard_map/ppermute | solution.py:257
  57.3 3.1 %first_step.9 = (f32[2,1,256,256]{3,2,1,0:T(8,128)}, f32[2,256,256]{2,1,0:T(8,128)S(1)}, f32[8,128]{1,0:T(8,128)S(1)}) custom-call(f32[2,8,256,256]{3,2,1,0:T(8,128)S(1)} %bitcast.67, f32[2,256,256]{2,1,0:T(8,128)S(1)} %collective-permute-done.3.a_ref, f32[2,256,256]{2,1,0:T(8,128)S(1)} %pad_maximum_fusion.1.q_ref, ...), custom_call_target="tpu_custom_call", output_to_operand_aliasing={{1}: (4, {}), {2}: (5, {})} | custom-call | flops 3000000000 | bytes 400000 | tf_op jit(solution)/shard_map/first_step/pallas_call | solution.py:176
  60.4 3.1 %first_step.10 = (f32[2,1,256,256]{3,2,1,0:T(8,128)}, f32[2,256,256]{2,1,0:T(8,128)S(1)}, f32[8,128]{1,0:T(8,128)S(1)}) custom-call(f32[2,2,256,256]{3,2,1,0:T(8,128)S(1)} %collective-permute-done.1.f_ref, f32[8,256,256]{2,1,0:T(8,128)S(1)} %bitcast.55, f32[2,256,256]{2,1,0:T(8,128)S(1)} %pad_maximum_fusion.q_ref, ...), custom_call_target="tpu_custom_call", output_to_operand_aliasing={{1}: (4, {}), {2}: (5, {})} | custom-call | flops 100000000 | bytes 400000 | tf_op jit(solution)/shard_map/first_step/pallas_call | solution.py:176
  63.5 0.6 collective-permute-start.8
  64.1 1.0 collective-permute-done.6
  65.1 3.5 %collective-permute-start.7 = (f32[2,1,256,256]{3,2,1,0:T(8,128)}, f32[2,1,256,256]{3,2,1,0:T(8,128)}, u32[]{:S(2)}, u32[]{:S(2)}) collective-permute-start(f32[2,1,256,256]{3,2,1,0:T(8,128)} %collective-permute-done.6), channel_id=1, source_target_pairs={{3,2},{0,3},{5,4},{6,5},{7,6},{4,7},{1,0},{2,1},{11,10},{8,11},{13... | collective-permute-start | bytes 1572872 | tf_op jit(solution)/shard_map/ppermute | solution.py:257
  68.6 3.1 %first_step.11 = (f32[2,1,256,256]{3,2,1,0:T(8,128)}, f32[2,256,256]{2,1,0:T(8,128)S(1)}, f32[8,128]{1,0:T(8,128)S(1)}) custom-call(f32[2,2,256,256]{3,2,1,0:T(8,128)S(1)} %collective-permute-done.1.f_ref, f32[8,256,256]{2,1,0:T(8,128)S(1)} %bitcast.56, f32[2,256,256]{2,1,0:T(8,128)S(1)} %pad_maximum_fusion.q_ref, ...), custom_call_target="tpu_custom_call", output_to_operand_aliasing={{1}: (4, {}), {2}: (5, {})} | custom-call | flops 5000000000 | bytes 400000 | tf_op jit(solution)/shard_map/first_step/pallas_call | solution.py:176
  71.7 3.3 %collective-permute-done.12.s_ref = f32[2,2,256,256]{3,2,1,0:T(8,128)S(1)} collective-permute-done((f32[2,2,256,256]{3,2,1,0:T(8,128)S(1)}, f32[2,2,256,256]{3,2,1,0:T(8,128)S(1)}, u32[]{:S(2)}, u32[]{:S(2)}) %collective-permute-start.12) | collective-permute-done | bytes 1048608 | tf_op jit(solution)/shard_map/ppermute | solution.py:257
  75.0 1.0 copy-done.9
  76.0 1.2 copy-done.3
  77.2 1.0 copy-done.5
  78.3 1.2 copy-done.10
  79.5 4.1 %second_step.6 = (f32[2,8,256,256]{3,2,1,0:T(8,128)}, f32[2,256,256]{2,1,0:T(8,128)S(1)}, f32[8,128]{1,0:T(8,128)S(1)}) custom-call(f32[2,2,256,256]{3,2,1,0:T(8,128)S(1)} %copy-done.10, f32[8,256,256]{2,1,0:T(8,128)S(1)} %bitcast.57, f32[2,256,256]{2,1,0:T(8,128)S(1)} %copy-done.5, ...), custom_call_target="tpu_custom_call", output_to_operand_aliasing={{1}: (4, {}), {2}: (5, {})} | custom-call | flops 100000000 | bytes 800000 | tf_op jit(solution)/shard_map/second_step/pallas_call | solution.py:176
  83.6 3.6 %collective-permute-done.11.s_ref = f32[2,1,256,256]{3,2,1,0:T(8,128)} collective-permute-done((f32[2,1,256,256]{3,2,1,0:T(8,128)}, f32[2,1,256,256]{3,2,1,0:T(8,128)}, u32[]{:S(2)}, u32[]{:S(2)}) %collective-permute-start.11) | collective-permute-done | bytes 524320 | tf_op jit(solution)/shard_map/ppermute | solution.py:257
  87.2 3.4 %second_step.7 = (f32[2,8,256,256]{3,2,1,0:T(8,128)}, f32[2,256,256]{2,1,0:T(8,128)S(1)}, f32[8,128]{1,0:T(8,128)S(1)}) custom-call(f32[2,1,256,256]{3,2,1,0:T(8,128)} %collective-permute-done.11.s_ref, f32[8,256,256]{2,1,0:T(8,128)S(1)} %bitcast.58, f32[2,256,256]{2,1,0:T(8,128)S(1)} %copy-done.5, ...), custom_call_target="tpu_custom_call", output_to_operand_aliasing={{1}: (4, {}), {2}: (5, {}), {0}: (6, {})} | custom-call | flops 100000000 | bytes 400000 | tf_op jit(solution)/shard_map/second_step/pallas_call | solution.py:176
  90.6 6.4 %collective-permute-done.10.s_ref = f32[2,2,256,256]{3,2,1,0:T(8,128)} collective-permute-done((f32[2,2,256,256]{3,2,1,0:T(8,128)}, f32[2,2,256,256]{3,2,1,0:T(8,128)}, u32[]{:S(2)}, u32[]{:S(2)}) %collective-permute-start.10) | collective-permute-done | bytes 1048608 | tf_op jit(solution)/shard_map/ppermute | solution.py:257
  97.0 5.1 %second_step.8 = (f32[2,8,256,256]{3,2,1,0:T(8,128)}, f32[2,256,256]{2,1,0:T(8,128)S(1)}, f32[8,128]{1,0:T(8,128)S(1)}) custom-call(f32[2,2,256,256]{3,2,1,0:T(8,128)} %collective-permute-done.10.s_ref, f32[8,256,256]{2,1,0:T(8,128)S(1)} %bitcast.59, f32[2,256,256]{2,1,0:T(8,128)S(1)} %copy-done.5, ...), custom_call_target="tpu_custom_call", output_to_operand_aliasing={{1}: (4, {}), {2}: (5, {}), {0}: (6, {})} | custom-call | flops 100000000 | bytes 800000 | tf_op jit(solution)/shard_map/second_step/pallas_call | solution.py:176
  102.1 3.4 %second_step.9 = (f32[2,8,256,256]{3,2,1,0:T(8,128)}, f32[2,256,256]{2,1,0:T(8,128)S(1)}, f32[8,128]{1,0:T(8,128)S(1)}) custom-call(f32[2,1,256,256]{3,2,1,0:T(8,128)} %collective-permute-done.8.s_ref, f32[8,256,256]{2,1,0:T(8,128)S(1)} %bitcast.60, f32[2,256,256]{2,1,0:T(8,128)S(1)} %copy-done.5, ...), custom_call_target="tpu_custom_call", output_to_operand_aliasing={{1}: (4, {}), {2}: (5, {}), {0}: (6, {})} | custom-call | flops 1000000000 | bytes 400000 | tf_op jit(solution)/shard_map/second_step/pallas_call | solution.py:176
  105.5 4.6 %collective-permute-done.7.s_ref = f32[2,1,256,256]{3,2,1,0:T(8,128)} collective-permute-done((f32[2,1,256,256]{3,2,1,0:T(8,128)}, f32[2,1,256,256]{3,2,1,0:T(8,128)}, u32[]{:S(2)}, u32[]{:S(2)}) %collective-permute-start.7) | collective-permute-done | bytes 524320 | tf_op jit(solution)/shard_map/ppermute | solution.py:257
  110.1 3.4 %second_step.10 = (f32[2,8,256,256]{3,2,1,0:T(8,128)}, f32[2,256,256]{2,1,0:T(8,128)S(1)}, f32[8,128]{1,0:T(8,128)S(1)}) custom-call(f32[2,1,256,256]{3,2,1,0:T(8,128)} %collective-permute-done.7.s_ref, f32[8,256,256]{2,1,0:T(8,128)S(1)} %bitcast.61, f32[2,256,256]{2,1,0:T(8,128)S(1)} %copy-done.5, ...), custom_call_target="tpu_custom_call", output_to_operand_aliasing={{1}: (4, {}), {2}: (5, {}), {0}: (6, {})} | custom-call | flops 1000000000 | bytes 400000 | tf_op jit(solution)/shard_map/second_step/pallas_call | solution.py:176
  113.6 3.5 %second_step.11 = (f32[2,8,256,256]{3,2,1,0:T(8,128)}, f32[2,256,256]{2,1,0:T(8,128)S(1)}, f32[8,128]{1,0:T(8,128)S(1)}) custom-call(f32[2,1,256,256]{3,2,1,0:T(8,128)} %collective-permute-done.5.s_ref, f32[8,256,256]{2,1,0:T(8,128)S(1)} %bitcast.62, f32[2,256,256]{2,1,0:T(8,128)S(1)} %copy-done.5, ...), custom_call_target="tpu_custom_call", output_to_operand_aliasing={{1}: (4, {}), {2}: (5, {}), {0}: (6, {})} | custom-call | flops 1000000000 | bytes 400000 | tf_op jit(solution)/shard_map/second_step/pallas_call | solution.py:176
  117.2 1.0 finish.1
  118.1 1.5 collective-permute-start.13
  119.6 1.2 collective-permute-done.13
  120.8 21.8 %all_to_all.11 = f32[64,8,128]{2,1,0:T(8,128)S(1)} all-to-all(f32[64,8,128]{2,1,0:T(8,128)S(1)} %bitcast.70), channel_id=1, replica_groups={{0,1,2,3,4,5,6,7,16,17,18,19,20,21,22,23,32,33,34,35,36,37,38,39,48,49,..., dimensions={0} | all-to-all | bytes 524288 | tf_op jit(solution)/shard_map/all_to_all | solution.py:235
  142.7 14.1 %all_to_all.10 = f32[64,8,128]{2,1,0:T(8,128)S(1)} all-to-all(f32[64,8,128]{2,1,0:T(8,128)S(1)} %broadcast_in_dim.18), channel_id=1, replica_groups={{0,1,2,3,4,5,6,7,16,17,18,19,20,21,22,23,32,33,34,35,36,37,38,39,48,49,..., dimensions={0} | all-to-all | bytes 524288 | tf_op jit(solution)/shard_map/all_to_all | solution.py:237
  156.8 3.2 %collective-permute-start.14 = (f32[2,256,128]{2,1,0:T(8,128)S(1)}, f32[2,256,128]{2,1,0:T(8,128)S(1)}, u32[]{:S(2)}, u32[]{:S(2)}) collective-permute-start(f32[2,256,128]{2,1,0:T(8,128)S(1)} %bitcast.71), channel_id=1, source_target_pairs={{0,8},{1,9},{2,10},{3,11},{4,12},{5,13},{6,14},{7,15},{8,0},{9,1},... | collective-permute-start | bytes 786440 | tf_op jit(solution)/shard_map/ppermute | solution.py:238
  160.0 1.2 collective-permute-done.14
  161.2 0.2 copy.43
  161.4 1.0 copy.45
  (49 shorter events, 0.6 us)
Async XLA Ops:
  0.6 8.7 %copy-start = (f32[2,256,256]{2,1,0:T(8,128)S(1)}, f32[2,256,256]{2,1,0:T(8,128)}, u32[]{:S(2)}) copy-start(f32[2,256,256]{2,1,0:T(8,128)} %param.12) | copy-start | bytes 1572868
  0.6 10.3 %copy-start.15 = (f32[256,256,1]{1,0,2:T(8,128)S(1)}, f32[256,256,1]{1,0,2:T(8,128)}, u32[]{:S(2)}) copy-start(f32[256,256,1]{1,0,2:T(8,128)} %constant.41) | copy-start | bytes 786436
  0.7 11.6 %copy-start.16 = (f32[256,256]{1,0:T(8,128)S(1)}, f32[256,256]{1,0:T(8,128)}, u32[]{:S(2)}) copy-start(f32[256,256]{1,0:T(8,128)} %constant.36.clone) | copy-start | bytes 786436
  0.7 11.6 %collective-permute-start = (f32[1]{0:T(128)}, f32[1]{0:T(128)}, u32[]{:S(2)}, u32[]{:S(2)}) collective-permute-start(f32[1]{0:T(128)} %param.13), channel_id=1, source_target_pairs={{0,1},{1,2},{2,3},{3,4},{4,5},{5,6},{6,7},{7,0},{8,9},{9,10},{10,1... | collective-permute-start | bytes 20 | tf_op jit(solution)/shard_map/ppermute | solution.py:257
  4.2 11.6 %copy-start.8 = (f32[2,1,8,256,256]{4,3,2,1,0:T(8,128)S(1)}, f32[2,1,8,256,256]{4,3,2,1,0:T(8,128)}, u32[]{:S(2)}) copy-start(f32[2,1,8,256,256]{4,3,2,1,0:T(8,128)} %param.10) | copy-start | bytes 12582916
  4.2 29.5 %collective-permute-start.2 = (f32[2,2,256,256]{3,2,1,0:T(8,128)S(1)}, f32[2,2,256,256]{3,2,1,0:T(8,128)S(1)}, u32[]{:S(2)}, u32[]{:S(2)}) collective-permute-start(f32[2,2,256,256]{3,2,1,0:T(8,128)S(1)} %slice.32), channel_id=1, source_target_pairs={{0,1},{1,2},{2,3},{3,4},{4,5},{5,6},{6,7},{7,0},{8,9},{9,10},{10,1... | collective-permute-start | bytes 3145736 | tf_op jit(solution)/shard_map/ppermute | solution.py:257
  6.6 9.4 %copy-start.1 = (f32[1,8,256,256]{3,2,1,0:T(8,128)S(1)}, f32[1,8,256,256]{3,2,1,0:T(8,128)}, u32[]{:S(2)}) copy-start(f32[1,8,256,256]{3,2,1,0:T(8,128)} %param.11) | copy-start | bytes 6291460
  6.6 13.1 %collective-permute-start.4 = (f32[2,256,256]{2,1,0:T(8,128)S(1)}, f32[2,256,256]{2,1,0:T(8,128)S(1)}, u32[]{:S(2)}, u32[]{:S(2)}) collective-permute-start(f32[2,256,256]{2,1,0:T(8,128)S(1)} %slice_bitcast_fusion), channel_id=1, source_target_pairs={{0,7},{1,0},{2,1},{3,2},{4,3},{5,4},{6,5},{7,6},{8,15},{9,8},{10,9... | collective-permute-start | bytes 1572872 | tf_op jit(solution)/shard_map/ppermute | solution.py:257
  12.3 7.6 %copy-start.2 = (bf16[2,4,256,256]{3,2,1,0:T(8,128)(2,1)S(1)}, bf16[2,4,256,256]{3,2,1,0:T(8,128)(2,1)}, u32[]{:S(2)}) copy-start(bf16[2,4,256,256]{3,2,1,0:T(8,128)(2,1)} %constant.34.clone.tables) | copy-start | bytes 3145732
  15.8 52.8 %copy-start.4 = (f32[2,256,256]{2,1,0:T(8,128)}, f32[2,256,256]{2,1,0:T(8,128)S(1)}, u32[]{:S(2)}) copy-start(f32[2,256,256]{2,1,0:T(8,128)S(1)} %pad_maximum_fusion.q_ref) | copy-start | bytes 1572868
  15.9 44.5 %collective-permute-start.1 = (f32[2,2,256,256]{3,2,1,0:T(8,128)S(1)}, f32[2,2,256,256]{3,2,1,0:T(8,128)S(1)}, u32[]{:S(2)}, u32[]{:S(2)}) collective-permute-start(f32[2,2,256,256]{3,2,1,0:T(8,128)S(1)} %slice.25), channel_id=1, source_target_pairs={{0,1},{1,2},{2,3},{3,4},{4,5},{5,6},{6,7},{7,0},{8,9},{9,10},{10,1... | collective-permute-start | bytes 3145736 | tf_op jit(solution)/shard_map/ppermute | solution.py:257
  16.1 15.3 %collective-permute-start.3 = (f32[2,256,256]{2,1,0:T(8,128)S(1)}, f32[2,256,256]{2,1,0:T(8,128)S(1)}, u32[]{:S(2)}, u32[]{:S(2)}) collective-permute-start(f32[2,256,256]{2,1,0:T(8,128)S(1)} %slice.27), channel_id=1, source_target_pairs={{0,7},{1,0},{2,1},{3,2},{4,3},{5,4},{6,5},{7,6},{8,15},{9,8},{10,9... | collective-permute-start | bytes 1572872 | tf_op jit(solution)/shard_map/ppermute | solution.py:257
  24.8 29.0 %collective-permute-start.9 = (f32[2,2,256,256]{3,2,1,0:T(8,128)S(1)}, f32[2,2,256,256]{3,2,1,0:T(8,128)}, u32[]{:S(2)}, u32[]{:S(2)}) collective-permute-start(f32[2,2,256,256]{3,2,1,0:T(8,128)S(1)} %get-tuple-element.57), channel_id=1, source_target_pairs={{0,3},{1,0},{2,5},{3,6},{4,7},{5,4},{6,1},{7,2},{8,11},{9,8},{10,1... | collective-permute-start | bytes 3145736 | tf_op jit(solution)/shard_map/ppermute | solution.py:257
  38.7 36.3 %collective-permute-start.12 = (f32[2,2,256,256]{3,2,1,0:T(8,128)S(1)}, f32[2,2,256,256]{3,2,1,0:T(8,128)S(1)}, u32[]{:S(2)}, u32[]{:S(2)}) collective-permute-start(f32[2,2,256,256]{3,2,1,0:T(8,128)S(1)} %get-tuple-element.59), channel_id=1, source_target_pairs={{0,1},{1,2},{2,3},{3,4},{4,5},{5,6},{6,7},{7,0},{8,9},{9,10},{10,1... | collective-permute-start | bytes 3145736 | tf_op jit(solution)/shard_map/ppermute | solution.py:257
  39.0 26.1 %collective-permute-start.6 = (f32[2,1,256,256]{3,2,1,0:T(8,128)S(1)}, f32[2,1,256,256]{3,2,1,0:T(8,128)}, u32[]{:S(2)}, u32[]{:S(2)}) collective-permute-start(f32[2,1,256,256]{3,2,1,0:T(8,128)S(1)} %get-tuple-element.55), channel_id=1, source_target_pairs={{0,3},{1,0},{2,5},{3,6},{4,7},{5,4},{6,1},{7,2},{8,11},{9,8},{10,1... | collective-permute-start | bytes 1572872 | tf_op jit(solution)/shard_map/ppermute | solution.py:257
  53.8 43.2 %collective-permute-start.10 = (f32[2,2,256,256]{3,2,1,0:T(8,128)}, f32[2,2,256,256]{3,2,1,0:T(8,128)}, u32[]{:S(2)}, u32[]{:S(2)}) collective-permute-start(f32[2,2,256,256]{3,2,1,0:T(8,128)} %collective-permute-done.9), channel_id=1, source_target_pairs={{3,2},{0,3},{5,4},{6,5},{7,6},{4,7},{1,0},{2,1},{11,10},{8,11},{13... | collective-permute-start | bytes 3145736 | tf_op jit(solution)/shard_map/ppermute | solution.py:257
  60.4 11.2 %copy-start.6 = (f32[2,256,256]{2,1,0:T(8,128)}, f32[2,256,256]{2,1,0:T(8,128)S(1)}, u32[]{:S(2)}) copy-start(f32[2,256,256]{2,1,0:T(8,128)S(1)} %get-tuple-element.79.b_ref) | copy-start | bytes 1572868
  60.4 26.8 %collective-permute-start.11 = (f32[2,1,256,256]{3,2,1,0:T(8,128)}, f32[2,1,256,256]{3,2,1,0:T(8,128)}, u32[]{:S(2)}, u32[]{:S(2)}) collective-permute-start(f32[2,1,256,256]{3,2,1,0:T(8,128)} %get-tuple-element.58), channel_id=1, source_target_pairs={{0,2},{1,3},{2,4},{3,5},{4,6},{5,7},{6,0},{7,1},{8,10},{9,11},{10,... | collective-permute-start | bytes 1572872 | tf_op jit(solution)/shard_map/ppermute | solution.py:257
  63.5 38.6 %collective-permute-start.8 = (f32[2,1,256,256]{3,2,1,0:T(8,128)}, f32[2,1,256,256]{3,2,1,0:T(8,128)}, u32[]{:S(2)}, u32[]{:S(2)}) collective-permute-start(f32[2,1,256,256]{3,2,1,0:T(8,128)} %get-tuple-element.56), channel_id=1, source_target_pairs={{0,1},{1,2},{2,3},{3,4},{4,5},{5,6},{6,7},{7,0},{8,9},{9,10},{10,1... | collective-permute-start | bytes 1572872 | tf_op jit(solution)/shard_map/ppermute | solution.py:257
  65.1 45.0 %collective-permute-start.7 = (f32[2,1,256,256]{3,2,1,0:T(8,128)}, f32[2,1,256,256]{3,2,1,0:T(8,128)}, u32[]{:S(2)}, u32[]{:S(2)}) collective-permute-start(f32[2,1,256,256]{3,2,1,0:T(8,128)} %collective-permute-done.6), channel_id=1, source_target_pairs={{3,2},{0,3},{5,4},{6,5},{7,6},{4,7},{1,0},{2,1},{11,10},{8,11},{13... | collective-permute-start | bytes 1572872 | tf_op jit(solution)/shard_map/ppermute | solution.py:257
  75.0 1.0 copy-start.9
  76.0 37.6 %collective-permute-start.5 = (f32[2,1,256,256]{3,2,1,0:T(8,128)}, f32[2,1,256,256]{3,2,1,0:T(8,128)}, u32[]{:S(2)}, u32[]{:S(2)}) collective-permute-start(f32[2,1,256,256]{3,2,1,0:T(8,128)} %get-tuple-element.54), channel_id=1, source_target_pairs={{0,1},{1,2},{2,3},{3,4},{4,5},{5,6},{6,7},{7,0},{8,9},{9,10},{10,1... | collective-permute-start | bytes 1572872 | tf_op jit(solution)/shard_map/ppermute | solution.py:257
  76.0 1.2 copy-start.3
  77.2 1.0 copy-start.5
  78.3 1.2 copy-start.10
  113.5 3.6 %copy-start.7 = (f32[2,256,256]{2,1,0:T(8,128)S(1)}, f32[2,256,256]{2,1,0:T(8,128)}, u32[]{:S(2)}) copy-start(f32[2,256,256]{2,1,0:T(8,128)} %copy-done.6) | copy-start | bytes 1572868
  113.5 3.6 %copy-start.11 = (f32[256,256]{1,0:T(8,128)S(1)}, f32[256,256]{1,0:T(8,128)}, u32[]{:S(2)}) copy-start(f32[256,256]{1,0:T(8,128)} %get-tuple-element.93.tb_re) | copy-start | bytes 786436
  113.6 3.6 %copy-start.12 = (f32[256,256]{1,0:T(8,128)S(1)}, f32[256,256]{1,0:T(8,128)}, u32[]{:S(2)}) copy-start(f32[256,256]{1,0:T(8,128)} %get-tuple-element.94.ta_im) | copy-start | bytes 786436
  113.6 3.6 %copy-start.13 = (f32[256,256]{1,0:T(8,128)S(1)}, f32[256,256]{1,0:T(8,128)}, u32[]{:S(2)}) copy-start(f32[256,256]{1,0:T(8,128)} %get-tuple-element.95.ta_re) | copy-start | bytes 786436
  113.6 3.6 %copy-start.14 = (bf16[2,256,256]{2,1,0:T(8,128)(2,1)S(1)}, bf16[2,256,256]{2,1,0:T(8,128)(2,1)}, u32[]{:S(2)}) copy-start(bf16[2,256,256]{2,1,0:T(8,128)(2,1)} %constant.37.clone.mix) | copy-start | bytes 786436
  118.1 2.6 %collective-permute-start.13 = (f32[2,256,128]{2,1,0:T(8,128)S(1)}, f32[2,256,128]{2,1,0:T(8,128)S(1)}, u32[]{:S(2)}, u32[]{:S(2)}) collective-permute-start(f32[2,256,128]{2,1,0:T(8,128)S(1)} %get-tuple-element.81), channel_id=1, source_target_pairs={{0,8},{1,9},{2,10},{3,11},{4,12},{5,13},{6,14},{7,15},{8,0},{9,1},... | collective-permute-start | bytes 786440 | tf_op jit(solution)/shard_map/ppermute | solution.py:234
  156.8 4.3 %collective-permute-start.14 = (f32[2,256,128]{2,1,0:T(8,128)S(1)}, f32[2,256,128]{2,1,0:T(8,128)S(1)}, u32[]{:S(2)}, u32[]{:S(2)}) collective-permute-start(f32[2,256,128]{2,1,0:T(8,128)S(1)} %bitcast.71), channel_id=1, source_target_pairs={{0,8},{1,9},{2,10},{3,11},{4,12},{5,13},{6,14},{7,15},{8,0},{9,1},... | collective-permute-start | bytes 786440 | tf_op jit(solution)/shard_map/ppermute | solution.py:238

commit v2 on v0

--- a/solution.py
+++ b/solution.py
@@ -146,6 +146,16 @@
     add(g_ref, grad_ref, *product_conj(w_re, w_im, s_re, s_im))
 
 
+def last_kernel(s_ref, a_ref, q_ref, tables, g_ref, other_ref, *rest):
+    first_one = pl.program_id(0) == 0
+
+    class Chosen:
+        def __getitem__(self, at):
+            return jnp.where(first_one, s_ref[at], other_ref[at])
+
+    second_kernel(Chosen(), a_ref, q_ref, tables, g_ref, *rest)
+
+
 def add(g_ref, grad_ref, g_re, g_im):
     @pl.when(pl.program_id(0) == 0)
     def _():
@@ -155,10 +165,10 @@
     grad_ref[1] += g_im
 
 
-def tile_spec(shape, at):
+def tile_spec(shape, at, stride=1):
     if len(shape) == 4:
-        return pl.BlockSpec((2, 1, WIDTH, WIDTH), lambda i: (0, at + i, 0, 0))
-    return pl.BlockSpec((1, WIDTH, WIDTH), lambda i: (at + i, 0, 0))
+        return pl.BlockSpec((2, 1, WIDTH, WIDTH), lambda i: (0, at + i * stride, 0, 0))
+    return pl.BlockSpec((1, WIDTH, WIDTH), lambda i: (at + i * stride, 0, 0))
 
 
 def whole(shape):
@@ -191,6 +201,37 @@
     )(x, amps, q, tables, grad, *more)
 
 
+def last_step(x, other, amps, at, other_at, q, tables, grad, token, out):
+    stride = other_at - at
+    return pl.pallas_call(
+        last_kernel,
+        grid=(2,),
+        in_specs=[whole(x.shape), tile_spec(amps.shape, at, stride), whole(PAIR), whole(tables.shape), whole(PAIR)]
+        + [whole(other.shape), ANY, ANY],
+        out_specs=[tile_spec(out.shape, at, stride), whole(PAIR), ANY],
+        out_shape=[jax.ShapeDtypeStruct(y.shape, F32) for y in (out, grad, token)],
+        input_output_aliases={4: 1, 6: 2, 7: 0},
+        compiler_params=pltpu.CompilerParams(vmem_limit_bytes=40 * 1024 * 1024),
+        cost_estimate=pl.CostEstimate(flops=1_000_000_000, bytes_accessed=800_000, transcendentals=0),
+        name="second_step",
+    )(x, amps, q, tables, grad, other, token, out)
+
+
+def laid_out(parts):
+    def kernel(in_ref, out_ref):
+        out_ref[0, :, :HALF] = in_ref[0, 0]
+        out_ref[0, :, HALF:] = in_ref[0, 1]
+
+    return pl.pallas_call(
+        kernel,
+        grid=(2,),
+        in_specs=[pl.BlockSpec((1, 2, WIDTH, HALF), lambda i: (i, 0, 0, 0))],
+        out_specs=pl.BlockSpec((1, WIDTH, WIDTH), lambda i: (i, 0, 0)),
+        out_shape=jax.ShapeDtypeStruct(PAIR, F32),
+        name="laid_out",
+    )(parts)
+
+
 def finish_kernel(a_ref, b_ref, ta_re, ta_im, tb_re, tb_im, mix, factor_ref, out_ref):
     a = product_conj(a_ref[0], a_ref[1], ta_re[...], ta_im[...])
     b = product_conj(b_ref[0], b_ref[1], tb_re[...], tb_im[...])
@@ -228,7 +269,7 @@
     mine = lax.all_to_all(mine, AXES, 0, 0, tiled=True).sum(0)
     mine = jnp.broadcast_to(mine[None], (members, *mine.shape))
     total = lax.all_to_all(mine, AXES, 0, 0, tiled=True).reshape(2, 2, WIDTH, HALF)
-    return total.transpose(0, 2, 1, 3).reshape(2, WIDTH, WIDTH)
+    return laid_out(total)
 
 
 def turned(distance):
@@ -291,8 +332,8 @@
     second(s_7, 7, 1, weights[6])
     second(s_45, 4, 2, weights[6])
     second(s_2, 2, 1, weights[7])
-    second(s_6, 6, 1, weights[7])
-    second(s_3, 3, 1, weights[7])
+    out, grads["before"], token = last_step(
+        s_6, s_3, amps, 6, 3, filters["before"], tables, grads["before"], token, out)
 
     parts = finished(grads["before"], grads["here"], turn_before, turn_here, mix, 2.0 * factor)
     return (out[:, None], summed(parts))

time: 161 us -> 161 us (level)
  waiting for transfers between devices: 42.2 us -> 47.8 us
  starting transfers between devices: 25.8 us -> 23.1 us
  blocking collectives: 43.5 us -> 41 us
    pallas_call x0 -> x2, Pallas kernels: none -> 5.87 us  [the longest x1 4.11 us: last_step(): pl.pallas_call(last_kernel, grid=(2,), in_specs=[whole(x.shape), tile_spe...]
    ppermute x13, waiting for transfers between devices: 42.2 us -> 47.8 us  [sent(): return lax.ppermute(value, 'plane', pairs)]
    pallas_call x12 -> x10, Pallas kernels: 37.4 us -> 32.6 us  [step_call(): pl.pallas_call(kernel, grid=(tiles,), in_specs=[tile_spec(x.shape, x_at),...]
    all_to_all x1, blocking collectives: 25.7 us -> 22.6 us  [summed(): mine = lax.all_to_all(mine, AXES, 0, 0, tiled=True).sum(0)]
    ppermute x13, starting transfers between devices: 25.8 us -> 23.1 us  [sent(): return lax.ppermute(value, 'plane', pairs)]
  transfers between devices with their start and end apart: 13 -> 13, of which waited for: 8 -> 9; matrix products, arithmetic and copies ran while one was open for 5% -> 5% of each run, Pallas kernels for 22% -> 20%
where the time goes in v2:
time: 161 us
  waiting for transfers between devices  47.8 us (30%)
  blocking collectives  41 us (25%)
  Pallas kernels  39.4 us (24%)
  starting transfers between devices  23.1 us (14%)
  other arithmetic  2.91 us (2%)
  local copies, waits for them, and re-layouts  2.79 us (2%)
  matrix products  2.34 us (1%)
    ppermute x13, waiting for transfers between devices, sent(): return lax.ppermute(value, 'plane', pairs)  47.8 us
    pallas_call x10, Pallas kernels, step_call(): pl.pallas_call(kernel, grid=(tiles,), in_specs=[tile_spec(x.shape, x_at),...  32.6 us
    ppermute x13, starting transfers between devices, sent(): return lax.ppermute(value, 'plane', pairs)  23.1 us
    all_to_all x1, blocking collectives, summed(): mine = lax.all_to_all(mine, AXES, 0, 0, tiled=True).sum(0)  22.6 us
    all_to_all x1, blocking collectives, summed(): lax.all_to_all(mine, AXES, 0, 0, tiled=True).reshape(2, 2, WIDTH, HALF)  18.4 us
    pallas_call x1, Pallas kernels, last_step(): pl.pallas_call(last_kernel, grid=(2,), in_specs=[whole(x.shape), tile_spe...  4.11 us
  transfers between devices with their start and end apart: 13, of which 9 were waited for; matrix products, arithmetic and copies ran while one was open for 5% of the time, Pallas kernels for 20%

profile of v2, /device:TPU:1, one launch (start us, length us, event | category | flops | bytes accessed | tf_op | source)
XLA Modules:
  0.0 160.9 jit_solution(18340531255875214573)
XLA Ops:
  0.6 0.0 copy-start
  0.6 0.0 copy-start.5
  0.7 0.0 copy-start.6
  0.7 2.2 %collective-permute-start = (f32[1]{0:T(128)}, f32[1]{0:T(128)}, u32[]{:S(2)}, u32[]{:S(2)}) collective-permute-start(f32[1]{0:T(128)} %param.13), channel_id=1, source_target_pairs={{0,1},{1,2},{2,3},{3,4},{4,5},{5,6},{6,7},{7,0},{8,9},{9,10},{10,1... | collective-permute-start | bytes 20 | tf_op jit(solution)/shard_map/ppermute | solution.py:289
  2.9 1.1 slice_bitcast_fusion
  3.9 2.9 %collective-permute-start.2 = (f32[2,256,256]{2,1,0:T(8,128)S(1)}, f32[2,256,256]{2,1,0:T(8,128)S(1)}, u32[]{:S(2)}, u32[]{:S(2)}) collective-permute-start(f32[2,256,256]{2,1,0:T(8,128)S(1)} %slice_bitcast_fusion), channel_id=1, source_target_pairs={{0,7},{1,0},{2,1},{3,2},{4,3},{5,4},{6,5},{7,6},{8,15},{9,8},{10,9... | collective-permute-start | bytes 1572872 | tf_op jit(solution)/shard_map/ppermute | solution.py:289
  6.9 1.4 slice.32
  8.3 0.0 copy-start.3
  8.4 0.1 collective-permute-start.6
  8.4 1.7 %convolution_bitcast_fusion = f32[2,256,256]{1,2,0:T(8,128)S(1)} fusion(f32[256,256,1]{1,0,2:T(8,128)} %constant.21, f32[2,256,256]{2,1,0:T(8,128)S(1)} %copy-done), kind=kOutput, calls=%fused_computation | convolution fusion | flops 402653184 | bytes 1310720 | tf_op jit(solution)/shard_map/ij,cjk,lk->cil/dot_general | solution.py:297
  10.2 0.6 fusion
  11.5 0.0 copy-start.2
  11.5 2.7 %subtract_bitcast_fusion = (f32[1,256,256]{2,1,0:T(8,128)S(1)}, f32[1,256,256]{2,1,0:T(8,128)S(1)}, f32[1,256,256]{2,1,0:T(8,128)S(1)}, f32[1,256,256]{2,1,0:T(8...) fusion(f32[2,256,256]{2,1,0:T(8,128)S(1)} %fusion, ...), kind=kLoop, calls=%fused_computation.11 | loop fusion | flops 917504 | bytes 2883592 | tf_op jit(solution)/shard_map/stack | solution.py:300
  14.3 3.5 %collective-permute-start.1 = (f32[2,256,256]{2,1,0:T(8,128)S(1)}, f32[2,256,256]{2,1,0:T(8,128)S(1)}, u32[]{:S(2)}, u32[]{:S(2)}) collective-permute-start(f32[2,256,256]{2,1,0:T(8,128)S(1)} %slice.25), channel_id=1, source_target_pairs={{0,7},{1,0},{2,1},{3,2},{4,3},{5,4},{6,5},{7,6},{8,15},{9,8},{10,9... | collective-permute-start | bytes 1572872 | tf_op jit(solution)/shard_map/ppermute | solution.py:289
  17.8 0.1 slice.28
  17.9 0.1 collective-permute-start.5
  18.1 5.0 %first_step.6 = (f32[2,2,256,256]{3,2,1,0:T(8,128)S(1)}, f32[2,256,256]{2,1,0:T(8,128)S(1)}, f32[8,128]{1,0:T(8,128)S(1)}) custom-call(f32[2,8,256,256]{3,2,1,0:T(8,128)S(1)} %bitcast.59, f32[2,256,256]{2,1,0:T(8,128)S(1)} %collective-permute-done.2.a_ref, f32[2,256,256]{2,1,0:T(8,128)S(1)} %pad_maximum_fusion.1.q_ref, ...), custom_call_target="tpu_custom_call", output_to_operand_aliasing={{1}: (4, {}), {2}: (5, {})} | custom-call | flops 30000001024 | bytes 800000 | tf_op jit(solution)/shard_map/first_step/pallas_call | solution.py:186
  23.1 3.5 %collective-permute-start.8 = (f32[2,2,256,256]{3,2,1,0:T(8,128)S(1)}, f32[2,2,256,256]{3,2,1,0:T(8,128)S(1)}, u32[]{:S(2)}, u32[]{:S(2)}) collective-permute-start(f32[2,2,256,256]{3,2,1,0:T(8,128)S(1)} %get-tuple-element.49), channel_id=1, source_target_pairs={{0,3},{1,0},{2,5},{3,6},{4,7},{5,4},{6,1},{7,2},{8,11},{9,8},{10,1... | collective-permute-start | bytes 3145736 | tf_op jit(solution)/shard_map/ppermute | solution.py:289
  26.5 1.9 %collective-permute-done.1.a_ref = f32[2,256,256]{2,1,0:T(8,128)S(1)} collective-permute-done((f32[2,256,256]{2,1,0:T(8,128)S(1)}, f32[2,256,256]{2,1,0:T(8,128)S(1)}, u32[]{:S(2)}, u32[]{:S(2)}) %collective-permute-start.1) | collective-permute-done | bytes 524320 | tf_op jit(solution)/shard_map/ppermute | solution.py:289
  28.5 2.4 %first_step.7 = (f32[2,1,256,256]{3,2,1,0:T(8,128)S(1)}, f32[2,256,256]{2,1,0:T(8,128)S(1)}, f32[8,128]{1,0:T(8,128)S(1)}) custom-call(f32[2,8,256,256]{3,2,1,0:T(8,128)S(1)} %bitcast.60, f32[2,256,256]{2,1,0:T(8,128)S(1)} %collective-permute-done.1.a_ref, f32[2,256,256]{2,1,0:T(8,128)S(1)} %pad_maximum_fusion.1.q_ref, ...), custom_call_target="tpu_custom_call", output_to_operand_aliasing={{1}: (4, {}), {2}: (5, {})} | custom-call | flops 3000000000 | bytes 400000 | tf_op jit(solution)/shard_map/first_step/pallas_call | solution.py:186
  30.8 3.4 %collective-permute-done.6.f_ref = f32[2,2,256,256]{3,2,1,0:T(8,128)S(1)} collective-permute-done((f32[2,2,256,256]{3,2,1,0:T(8,128)S(1)}, f32[2,2,256,256]{3,2,1,0:T(8,128)S(1)}, u32[]{:S(2)}, u32[]{:S(2)}) %collective-permute-start.6) | collective-permute-done | bytes 1048608 | tf_op jit(solution)/shard_map/ppermute | solution.py:289
  34.3 5.0 %first_step.8 = (f32[2,2,256,256]{3,2,1,0:T(8,128)S(1)}, f32[2,256,256]{2,1,0:T(8,128)S(1)}, f32[8,128]{1,0:T(8,128)S(1)}) custom-call(f32[2,2,256,256]{3,2,1,0:T(8,128)S(1)} %collective-permute-done.6.f_ref, f32[8,256,256]{2,1,0:T(8,128)S(1)} %bitcast.48, f32[2,256,256]{2,1,0:T(8,128)S(1)} %pad_maximum_fusion.q_ref, ...), custom_call_target="tpu_custom_call", output_to_operand_aliasing={{1}: (4, {}), {2}: (5, {})} | custom-call | flops 30000001024 | bytes 800000 | tf_op jit(solution)/shard_map/first_step/pallas_call | solution.py:186
  39.3 0.1 collective-permute-start.11
  39.4 3.1 %collective-permute-start.3 = (f32[2,1,256,256]{3,2,1,0:T(8,128)S(1)}, f32[2,1,256,256]{3,2,1,0:T(8,128)S(1)}, u32[]{:S(2)}, u32[]{:S(2)}) collective-permute-start(f32[2,1,256,256]{3,2,1,0:T(8,128)S(1)} %get-tuple-element.40), channel_id=1, source_target_pairs={{0,3},{1,0},{2,5},{3,6},{4,7},{5,4},{6,1},{7,2},{8,11},{9,8},{10,1... | collective-permute-start | bytes 1572872 | tf_op jit(solution)/shard_map/ppermute | solution.py:289
  42.5 8.4 %collective-permute-done.8 = f32[2,2,256,256]{3,2,1,0:T(8,128)S(1)} collective-permute-done((f32[2,2,256,256]{3,2,1,0:T(8,128)S(1)}, f32[2,2,256,256]{3,2,1,0:T(8,128)S(1)}, u32[]{:S(2)}, u32[]{:S(2)}) %collective-permute-start.8) | collective-permute-done | bytes 1048608 | tf_op jit(solution)/shard_map/ppermute | solution.py:289
  50.9 3.4 %collective-permute-start.9 = (f32[2,2,256,256]{3,2,1,0:T(8,128)S(1)}, f32[2,2,256,256]{3,2,1,0:T(8,128)S(1)}, u32[]{:S(2)}, u32[]{:S(2)}) collective-permute-start(f32[2,2,256,256]{3,2,1,0:T(8,128)S(1)} %collective-permute-done.8), channel_id=1, source_target_pairs={{3,2},{0,3},{5,4},{6,5},{7,6},{4,7},{1,0},{2,1},{11,10},{8,11},{13... | collective-permute-start | bytes 3145736 | tf_op jit(solution)/shard_map/ppermute | solution.py:289
  54.3 2.4 %first_step.9 = (f32[2,1,256,256]{3,2,1,0:T(8,128)S(1)}, f32[2,256,256]{2,1,0:T(8,128)S(1)}, f32[8,128]{1,0:T(8,128)S(1)}) custom-call(f32[2,8,256,256]{3,2,1,0:T(8,128)S(1)} %bitcast.61, f32[2,256,256]{2,1,0:T(8,128)S(1)} %collective-permute-done.1.a_ref, f32[2,256,256]{2,1,0:T(8,128)S(1)} %pad_maximum_fusion.1.q_ref, ...), custom_call_target="tpu_custom_call", output_to_operand_aliasing={{1}: (4, {}), {2}: (5, {})} | custom-call | flops 3000000000 | bytes 400000 | tf_op jit(solution)/shard_map/first_step/pallas_call | solution.py:186
  56.7 0.4 collective-permute-start.10
  57.1 2.4 %first_step.10 = (f32[2,1,256,256]{3,2,1,0:T(8,128)S(1)}, f32[2,256,256]{2,1,0:T(8,128)S(1)}, f32[8,128]{1,0:T(8,128)S(1)}) custom-call(f32[2,2,256,256]{3,2,1,0:T(8,128)S(1)} %collective-permute-done.5.f_ref, f32[8,256,256]{2,1,0:T(8,128)S(1)} %bitcast.49, f32[2,256,256]{2,1,0:T(8,128)S(1)} %pad_maximum_fusion.q_ref, ...), custom_call_target="tpu_custom_call", output_to_operand_aliasing={{1}: (4, {}), {2}: (5, {})} | custom-call | flops 100000000 | bytes 400000 | tf_op jit(solution)/shard_map/first_step/pallas_call | solution.py:186
  59.5 0.5 collective-permute-start.7
  59.9 2.2 %collective-permute-done.3 = f32[2,1,256,256]{3,2,1,0:T(8,128)S(1)} collective-permute-done((f32[2,1,256,256]{3,2,1,0:T(8,128)S(1)}, f32[2,1,256,256]{3,2,1,0:T(8,128)S(1)}, u32[]{:S(2)}, u32[]{:S(2)}) %collective-permute-start.3) | collective-permute-done | bytes 524320 | tf_op jit(solution)/shard_map/ppermute | solution.py:289
  62.2 3.4 %collective-permute-start.4 = (f32[2,1,256,256]{3,2,1,0:T(8,128)S(1)}, f32[2,1,256,256]{3,2,1,0:T(8,128)S(1)}, u32[]{:S(2)}, u32[]{:S(2)}) collective-permute-start(f32[2,1,256,256]{3,2,1,0:T(8,128)S(1)} %collective-permute-done.3), channel_id=1, source_target_pairs={{3,2},{0,3},{5,4},{6,5},{7,6},{4,7},{1,0},{2,1},{11,10},{8,11},{13... | collective-permute-start | bytes 1572872 | tf_op jit(solution)/shard_map/ppermute | solution.py:289
  65.6 2.4 %first_step.11 = (f32[2,1,256,256]{3,2,1,0:T(8,128)S(1)}, f32[2,256,256]{2,1,0:T(8,128)S(1)}, f32[8,128]{1,0:T(8,128)S(1)}) custom-call(f32[2,2,256,256]{3,2,1,0:T(8,128)S(1)} %collective-permute-done.5.f_ref, f32[8,256,256]{2,1,0:T(8,128)S(1)} %bitcast.50, f32[2,256,256]{2,1,0:T(8,128)S(1)} %pad_maximum_fusion.q_ref, ...), custom_call_target="tpu_custom_call", output_to_operand_aliasing={{1}: (4, {}), {2}: (5, {})} | custom-call | flops 5000000000 | bytes 400000 | tf_op jit(solution)/shard_map/first_step/pallas_call | solution.py:186
  68.0 12.5 %collective-permute-done.11.s_ref = f32[2,2,256,256]{3,2,1,0:T(8,128)S(1)} collective-permute-done((f32[2,2,256,256]{3,2,1,0:T(8,128)S(1)}, f32[2,2,256,256]{3,2,1,0:T(8,128)S(1)}, u32[]{:S(2)}, u32[]{:S(2)}) %collective-permute-start.11) | collective-permute-done | bytes 1048608 | tf_op jit(solution)/shard_map/ppermute | solution.py:289
  80.5 4.2 %second_step.5 = (f32[2,8,256,256]{3,2,1,0:T(8,128)}, f32[2,256,256]{2,1,0:T(8,128)S(1)}, f32[8,128]{1,0:T(8,128)S(1)}) custom-call(f32[2,2,256,256]{3,2,1,0:T(8,128)S(1)} %collective-permute-done.11.s_ref, f32[8,256,256]{2,1,0:T(8,128)S(1)} %bitcast.51, f32[2,256,256]{2,1,0:T(8,128)S(1)} %pad_maximum_fusion.q_ref, ...), custom_call_target="tpu_custom_call", output_to_operand_aliasing={{1}: (4, {}), {2}: (5, {})} | custom-call | flops 100000000 | bytes 800000 | tf_op jit(solution)/shard_map/second_step/pallas_call | solution.py:186
  84.6 4.5 %collective-permute-done.10.s_ref = f32[2,1,256,256]{3,2,1,0:T(8,128)S(1)} collective-permute-done((f32[2,1,256,256]{3,2,1,0:T(8,128)S(1)}, f32[2,1,256,256]{3,2,1,0:T(8,128)S(1)}, u32[]{:S(2)}, u32[]{:S(2)}) %collective-permute-start.10) | collective-permute-done | bytes 524320 | tf_op jit(solution)/shard_map/ppermute | solution.py:289
  89.2 2.4 %second_step.6 = (f32[2,8,256,256]{3,2,1,0:T(8,128)}, f32[2,256,256]{2,1,0:T(8,128)S(1)}, f32[8,128]{1,0:T(8,128)S(1)}) custom-call(f32[2,1,256,256]{3,2,1,0:T(8,128)S(1)} %collective-permute-done.10.s_ref, f32[8,256,256]{2,1,0:T(8,128)S(1)} %bitcast.52, ...), custom_call_target="tpu_custom_call", output_to_operand_aliasing={{1}: (4, {}), {2}: (5, {}), {0}: (6, {})} | custom-call | flops 100000000 | bytes 400000 | tf_op jit(solution)/shard_map/second_step/pallas_call | solution.py:186
  91.6 4.2 %second_step.7 = (f32[2,8,256,256]{3,2,1,0:T(8,128)}, f32[2,256,256]{2,1,0:T(8,128)S(1)}, f32[8,128]{1,0:T(8,128)S(1)}) custom-call(f32[2,2,256,256]{3,2,1,0:T(8,128)S(1)} %collective-permute-done.9.s_ref, f32[8,256,256]{2,1,0:T(8,128)S(1)} %bitcast.53, ...), custom_call_target="tpu_custom_call", output_to_operand_aliasing={{1}: (4, {}), {2}: (5, {}), {0}: (6, {})} | custom-call | flops 100000000 | bytes 800000 | tf_op jit(solution)/shard_map/second_step/pallas_call | solution.py:186
  95.7 5.9 %collective-permute-done.7.s_ref = f32[2,1,256,256]{3,2,1,0:T(8,128)S(1)} collective-permute-done((f32[2,1,256,256]{3,2,1,0:T(8,128)S(1)}, f32[2,1,256,256]{3,2,1,0:T(8,128)S(1)}, u32[]{:S(2)}, u32[]{:S(2)}) %collective-permute-start.7) | collective-permute-done | bytes 524320 | tf_op jit(solution)/shard_map/ppermute | solution.py:289
  101.7 2.4 %second_step.8 = (f32[2,8,256,256]{3,2,1,0:T(8,128)}, f32[2,256,256]{2,1,0:T(8,128)S(1)}, f32[8,128]{1,0:T(8,128)S(1)}) custom-call(f32[2,1,256,256]{3,2,1,0:T(8,128)S(1)} %collective-permute-done.7.s_ref, f32[8,256,256]{2,1,0:T(8,128)S(1)} %bitcast.54, ...), custom_call_target="tpu_custom_call", output_to_operand_aliasing={{1}: (4, {}), {2}: (5, {}), {0}: (6, {})} | custom-call | flops 1000000000 | bytes 400000 | tf_op jit(solution)/shard_map/second_step/pallas_call | solution.py:186
  104.1 3.0 %collective-permute-done.4.s_ref = f32[2,1,256,256]{3,2,1,0:T(8,128)S(1)} collective-permute-done((f32[2,1,256,256]{3,2,1,0:T(8,128)S(1)}, f32[2,1,256,256]{3,2,1,0:T(8,128)S(1)}, u32[]{:S(2)}, u32[]{:S(2)}) %collective-permute-start.4) | collective-permute-done | bytes 524320 | tf_op jit(solution)/shard_map/ppermute | solution.py:289
  107.1 5.8 %collective-permute-done.12.other_ref = f32[2,1,256,256]{3,2,1,0:T(8,128)S(1)} collective-permute-done((f32[2,1,256,256]{3,2,1,0:T(8,128)S(1)}, f32[2,1,256,256]{3,2,1,0:T(8,128)S(1)}, u32[]{:S(2)}, u32[]{:S(2)}) %collective-permute-start.12) | collective-permute-done | bytes 524320 | tf_op jit(solution)/shard_map/ppermute | solution.py:289
  112.9 4.1 %second_step.9 = (f32[2,8,256,256]{3,2,1,0:T(8,128)}, f32[2,256,256]{2,1,0:T(8,128)S(1)}, f32[8,128]{1,0:T(8,128)S(1)}) custom-call(f32[2,1,256,256]{3,2,1,0:T(8,128)S(1)} %collective-permute-done.4.s_ref, f32[8,256,256]{2,1,0:T(8,128)S(1)} %bitcast.55, ...), custom_call_target="tpu_custom_call", output_to_operand_aliasing={{1}: (4, {}), {2}: (6, {}), {0}: (7, {})} | custom-call | flops 1000000000 | bytes 800000 | tf_op jit(solution)/shard_map/second_step/pallas_call | solution.py:206
  117.0 0.9 finish.1
  118.0 22.6 %all_to_all.11 = f32[128,8,128]{2,1,0:T(8,128)S(1)} all-to-all(f32[128,8,128]{2,1,0:T(8,128)S(1)} %bitcast.56), channel_id=1, replica_groups=mesh['tile'=16,'plane'=8] {'tile','plane'}, dimensions={0} | all-to-all | bytes 1048576 | tf_op jit(solution)/shard_map/all_to_all | solution.py:269
  140.5 0.1 reduce_sum.9
  140.7 18.4 %all_to_all.10 = f32[128,8,128]{2,1,0:T(8,128)} all-to-all(f32[128,8,128]{2,1,0:T(8,128)S(1)} %broadcast_in_dim.14), channel_id=1, replica_groups=mesh['tile'=16,'plane'=8] {'tile','plane'}, dimensions={0} | all-to-all | bytes 1048576 | tf_op jit(solution)/shard_map/all_to_all | solution.py:271
  159.1 1.8 %laid_out.1 = f32[2,256,256]{2,1,0:T(8,128)} custom-call(f32[2,2,256,128]{3,2,1,0:T(8,128)} %bitcast.63), custom_call_target="tpu_custom_call" | custom-call | tf_op jit(solution)/shard_map/laid_out/pallas_call | solution.py:225
  (21 shorter events, 0.3 us)
Async XLA Ops:
  0.6 7.8 %copy-start = (f32[2,256,256]{2,1,0:T(8,128)S(1)}, f32[2,256,256]{2,1,0:T(8,128)}, u32[]{:S(2)}) copy-start(f32[2,256,256]{2,1,0:T(8,128)} %param.12) | copy-start | bytes 1572868
  0.6 9.5 %copy-start.5 = (f32[256,256,1]{1,0,2:T(8,128)S(1)}, f32[256,256,1]{1,0,2:T(8,128)}, u32[]{:S(2)}) copy-start(f32[256,256,1]{1,0,2:T(8,128)} %constant.21) | copy-start | bytes 786436
  0.7 10.8 %copy-start.6 = (f32[256,256]{1,0:T(8,128)S(1)}, f32[256,256]{1,0:T(8,128)}, u32[]{:S(2)}) copy-start(f32[256,256]{1,0:T(8,128)} %constant.16.clone) | copy-start | bytes 786436
  0.7 10.8 %collective-permute-start = (f32[1]{0:T(128)}, f32[1]{0:T(128)}, u32[]{:S(2)}, u32[]{:S(2)}) collective-permute-start(f32[1]{0:T(128)} %param.13), channel_id=1, source_target_pairs={{0,1},{1,2},{2,3},{3,4},{4,5},{5,6},{6,7},{7,0},{8,9},{9,10},{10,1... | collective-permute-start | bytes 20 | tf_op jit(solution)/shard_map/ppermute | solution.py:289
  3.9 14.0 %collective-permute-start.2 = (f32[2,256,256]{2,1,0:T(8,128)S(1)}, f32[2,256,256]{2,1,0:T(8,128)S(1)}, u32[]{:S(2)}, u32[]{:S(2)}) collective-permute-start(f32[2,256,256]{2,1,0:T(8,128)S(1)} %slice_bitcast_fusion), channel_id=1, source_target_pairs={{0,7},{1,0},{2,1},{3,2},{4,3},{5,4},{6,5},{7,6},{8,15},{9,8},{10,9... | collective-permute-start | bytes 1572872 | tf_op jit(solution)/shard_map/ppermute | solution.py:289
  6.9 7.4 %copy-start.1 = (f32[1,8,256,256]{3,2,1,0:T(8,128)S(1)}, f32[1,8,256,256]{3,2,1,0:T(8,128)}, u32[]{:S(2)}) copy-start(f32[1,8,256,256]{3,2,1,0:T(8,128)} %param.11) | copy-start | bytes 6291460
  8.3 9.4 %copy-start.3 = (f32[2,1,8,256,256]{4,3,2,1,0:T(8,128)S(1)}, f32[2,1,8,256,256]{4,3,2,1,0:T(8,128)}, u32[]{:S(2)}) copy-start(f32[2,1,8,256,256]{4,3,2,1,0:T(8,128)} %param.10) | copy-start | bytes 12582916
  8.4 25.9 %collective-permute-start.6 = (f32[2,2,256,256]{3,2,1,0:T(8,128)S(1)}, f32[2,2,256,256]{3,2,1,0:T(8,128)S(1)}, u32[]{:S(2)}, u32[]{:S(2)}) collective-permute-start(f32[2,2,256,256]{3,2,1,0:T(8,128)S(1)} %slice.32), channel_id=1, source_target_pairs={{0,1},{1,2},{2,3},{3,4},{4,5},{5,6},{6,7},{7,0},{8,9},{9,10},{10,1... | collective-permute-start | bytes 3145736 | tf_op jit(solution)/shard_map/ppermute | solution.py:289
  11.5 6.6 %copy-start.2 = (bf16[2,4,256,256]{3,2,1,0:T(8,128)(2,1)S(1)}, bf16[2,4,256,256]{3,2,1,0:T(8,128)(2,1)}, u32[]{:S(2)}) copy-start(bf16[2,4,256,256]{3,2,1,0:T(8,128)(2,1)} %constant.4.clone.tables) | copy-start | bytes 3145732
  14.3 14.2 %collective-permute-start.1 = (f32[2,256,256]{2,1,0:T(8,128)S(1)}, f32[2,256,256]{2,1,0:T(8,128)S(1)}, u32[]{:S(2)}, u32[]{:S(2)}) collective-permute-start(f32[2,256,256]{2,1,0:T(8,128)S(1)} %slice.25), channel_id=1, source_target_pairs={{0,7},{1,0},{2,1},{3,2},{4,3},{5,4},{6,5},{7,6},{8,15},{9,8},{10,9... | collective-permute-start | bytes 1572872 | tf_op jit(solution)/shard_map/ppermute | solution.py:289
  17.9 39.2 %collective-permute-start.5 = (f32[2,2,256,256]{3,2,1,0:T(8,128)S(1)}, f32[2,2,256,256]{3,2,1,0:T(8,128)S(1)}, u32[]{:S(2)}, u32[]{:S(2)}) collective-permute-start(f32[2,2,256,256]{3,2,1,0:T(8,128)S(1)} %slice.28), channel_id=1, source_target_pairs={{0,1},{1,2},{2,3},{3,4},{4,5},{5,6},{6,7},{7,0},{8,9},{9,10},{10,1... | collective-permute-start | bytes 3145736 | tf_op jit(solution)/shard_map/ppermute | solution.py:289
  23.1 27.9 %collective-permute-start.8 = (f32[2,2,256,256]{3,2,1,0:T(8,128)S(1)}, f32[2,2,256,256]{3,2,1,0:T(8,128)S(1)}, u32[]{:S(2)}, u32[]{:S(2)}) collective-permute-start(f32[2,2,256,256]{3,2,1,0:T(8,128)S(1)} %get-tuple-element.49), channel_id=1, source_target_pairs={{0,3},{1,0},{2,5},{3,6},{4,7},{5,4},{6,1},{7,2},{8,11},{9,8},{10,1... | collective-permute-start | bytes 3145736 | tf_op jit(solution)/shard_map/ppermute | solution.py:289
  39.3 41.2 %collective-permute-start.11 = (f32[2,2,256,256]{3,2,1,0:T(8,128)S(1)}, f32[2,2,256,256]{3,2,1,0:T(8,128)S(1)}, u32[]{:S(2)}, u32[]{:S(2)}) collective-permute-start(f32[2,2,256,256]{3,2,1,0:T(8,128)S(1)} %get-tuple-element.51), channel_id=1, source_target_pairs={{0,1},{1,2},{2,3},{3,4},{4,5},{5,6},{6,7},{7,0},{8,9},{9,10},{10,1... | collective-permute-start | bytes 3145736 | tf_op jit(solution)/shard_map/ppermute | solution.py:289
  39.4 22.8 %collective-permute-start.3 = (f32[2,1,256,256]{3,2,1,0:T(8,128)S(1)}, f32[2,1,256,256]{3,2,1,0:T(8,128)S(1)}, u32[]{:S(2)}, u32[]{:S(2)}) collective-permute-start(f32[2,1,256,256]{3,2,1,0:T(8,128)S(1)} %get-tuple-element.40), channel_id=1, source_target_pairs={{0,3},{1,0},{2,5},{3,6},{4,7},{5,4},{6,1},{7,2},{8,11},{9,8},{10,1... | collective-permute-start | bytes 1572872 | tf_op jit(solution)/shard_map/ppermute | solution.py:289
  50.9 40.6 %collective-permute-start.9 = (f32[2,2,256,256]{3,2,1,0:T(8,128)S(1)}, f32[2,2,256,256]{3,2,1,0:T(8,128)S(1)}, u32[]{:S(2)}, u32[]{:S(2)}) collective-permute-start(f32[2,2,256,256]{3,2,1,0:T(8,128)S(1)} %collective-permute-done.8), channel_id=1, source_target_pairs={{3,2},{0,3},{5,4},{6,5},{7,6},{4,7},{1,0},{2,1},{11,10},{8,11},{13... | collective-permute-start | bytes 3145736 | tf_op jit(solution)/shard_map/ppermute | solution.py:289
  56.7 32.4 %collective-permute-start.10 = (f32[2,1,256,256]{3,2,1,0:T(8,128)S(1)}, f32[2,1,256,256]{3,2,1,0:T(8,128)S(1)}, u32[]{:S(2)}, u32[]{:S(2)}) collective-permute-start(f32[2,1,256,256]{3,2,1,0:T(8,128)S(1)} %get-tuple-element.50), channel_id=1, source_target_pairs={{0,2},{1,3},{2,4},{3,5},{4,6},{5,7},{6,0},{7,1},{8,10},{9,11},{10,... | collective-permute-start | bytes 1572872 | tf_op jit(solution)/shard_map/ppermute | solution.py:289
  59.5 42.2 %collective-permute-start.7 = (f32[2,1,256,256]{3,2,1,0:T(8,128)S(1)}, f32[2,1,256,256]{3,2,1,0:T(8,128)S(1)}, u32[]{:S(2)}, u32[]{:S(2)}) collective-permute-start(f32[2,1,256,256]{3,2,1,0:T(8,128)S(1)} %get-tuple-element.48), channel_id=1, source_target_pairs={{0,1},{1,2},{2,3},{3,4},{4,5},{5,6},{6,7},{7,0},{8,9},{9,10},{10,1... | collective-permute-start | bytes 1572872 | tf_op jit(solution)/shard_map/ppermute | solution.py:289
  62.2 44.9 %collective-permute-start.4 = (f32[2,1,256,256]{3,2,1,0:T(8,128)S(1)}, f32[2,1,256,256]{3,2,1,0:T(8,128)S(1)}, u32[]{:S(2)}, u32[]{:S(2)}) collective-permute-start(f32[2,1,256,256]{3,2,1,0:T(8,128)S(1)} %collective-permute-done.3), channel_id=1, source_target_pairs={{3,2},{0,3},{5,4},{6,5},{7,6},{4,7},{1,0},{2,1},{11,10},{8,11},{13... | collective-permute-start | bytes 1572872 | tf_op jit(solution)/shard_map/ppermute | solution.py:289
  80.5 32.4 %collective-permute-start.12 = (f32[2,1,256,256]{3,2,1,0:T(8,128)S(1)}, f32[2,1,256,256]{3,2,1,0:T(8,128)S(1)}, u32[]{:S(2)}, u32[]{:S(2)}) collective-permute-start(f32[2,1,256,256]{3,2,1,0:T(8,128)S(1)} %get-tuple-element.66), channel_id=1, source_target_pairs={{0,1},{1,2},{2,3},{3,4},{4,5},{5,6},{6,7},{7,0},{8,9},{9,10},{10,1... | collective-permute-start | bytes 1572872 | tf_op jit(solution)/shard_map/ppermute | solution.py:289
  112.9 4.1 %copy-start.4 = (bf16[2,256,256]{2,1,0:T(8,128)(2,1)S(1)}, bf16[2,256,256]{2,1,0:T(8,128)(2,1)}, u32[]{:S(2)}) copy-start(bf16[2,256,256]{2,1,0:T(8,128)(2,1)} %constant.17.clone.mix) | copy-start | bytes 786436

commit v3 on v2

--- a/solution.py
+++ b/solution.py
@@ -217,21 +217,6 @@
     )(x, amps, q, tables, grad, other, token, out)
 
 
-def laid_out(parts):
-    def kernel(in_ref, out_ref):
-        out_ref[0, :, :HALF] = in_ref[0, 0]
-        out_ref[0, :, HALF:] = in_ref[0, 1]
-
-    return pl.pallas_call(
-        kernel,
-        grid=(2,),
-        in_specs=[pl.BlockSpec((1, 2, WIDTH, HALF), lambda i: (i, 0, 0, 0))],
-        out_specs=pl.BlockSpec((1, WIDTH, WIDTH), lambda i: (i, 0, 0)),
-        out_shape=jax.ShapeDtypeStruct(PAIR, F32),
-        name="laid_out",
-    )(parts)
-
-
 def finish_kernel(a_ref, b_ref, ta_re, ta_im, tb_re, tb_im, mix, factor_ref, out_ref):
     a = product_conj(a_ref[0], a_ref[1], ta_re[...], ta_im[...])
     b = product_conj(b_ref[0], b_ref[1], tb_re[...], tb_im[...])
@@ -269,7 +254,7 @@
     mine = lax.all_to_all(mine, AXES, 0, 0, tiled=True).sum(0)
     mine = jnp.broadcast_to(mine[None], (members, *mine.shape))
     total = lax.all_to_all(mine, AXES, 0, 0, tiled=True).reshape(2, 2, WIDTH, HALF)
-    return laid_out(total)
+    return total.transpose(0, 2, 1, 3).reshape(2, WIDTH, WIDTH)
 
 
 def turned(distance):
@@ -319,7 +304,7 @@
         out, grads["before"], token = step_call(
             second_kernel, x, 0, amps, at, filters["before"], tables, grads["before"], token, tiles, out, at, count, (), weight, "second_step")
 
-    weights = [30, 3, 30, 3, 0.1, 5, 0.1, 1]
+    weights = [5, 30, 3, 1, 0.1, 5, 3, 10]
     s_45 = sent(first("here", fields, 4, amps_45, 0, 2, weights[0]), back)
     s_6 = sent(first("here", fields, 6, amps_67, 0, 1, weights[1]), back)
     s_01 = sent(first("before", fields_01, 0, amps, 0, 2, weights[2]), ahead)

time: 161 us -> 160 us (level)
  starting transfers between devices: 23.1 us -> 29.1 us
  waiting for transfers between devices: 47.8 us -> 41.9 us
  Pallas kernels: 39.4 us -> 37.6 us
    ppermute x13, starting transfers between devices: 23.1 us -> 29.1 us  [sent(): return lax.ppermute(value, 'plane', pairs)]
    ppermute x13, waiting for transfers between devices: 47.8 us -> 41.9 us  [sent(): return lax.ppermute(value, 'plane', pairs)]
    pallas_call x1 -> x0, Pallas kernels: 1.76 us -> none  [laid_out(): pl.pallas_call(kernel, grid=(2,), in_specs=[pl.BlockSpec((1, 2, WIDTH, HA...]
  transfers between devices with their start and end apart: 13 -> 13, of which waited for: 9 -> 7; matrix products, arithmetic and copies ran while one was open for 5% -> 5% of each run, Pallas kernels for 20% -> 20%
where the time goes in v3:
time: 160 us
  waiting for transfers between devices  41.9 us (26%)
  blocking collectives  40.4 us (25%)
  Pallas kernels  37.6 us (24%)
  starting transfers between devices  29.1 us (18%)
  local copies, waits for them, and re-layouts  3.99 us (2%)
  other arithmetic  2.91 us (2%)
  matrix products  2.33 us (1%)
    ppermute x13, waiting for transfers between devices, sent(): return lax.ppermute(value, 'plane', pairs)  41.9 us
    pallas_call x10, Pallas kernels, step_call(): pl.pallas_call(kernel, grid=(tiles,), in_specs=[tile_spec(x.shape, x_at),...  32.5 us
    ppermute x13, starting transfers between devices, sent(): return lax.ppermute(value, 'plane', pairs)  29.1 us
    all_to_all x1, blocking collectives, summed(): mine = lax.all_to_all(mine, AXES, 0, 0, tiled=True).sum(0)  22.6 us
    all_to_all x1, blocking collectives, summed(): lax.all_to_all(mine, AXES, 0, 0, tiled=True).reshape(2, 2, WIDTH, HALF)  17.8 us
    pallas_call x1, Pallas kernels, last_step(): pl.pallas_call(last_kernel, grid=(2,), in_specs=[whole(x.shape), tile_spe...  4.11 us
  transfers between devices with their start and end apart: 13, of which 7 were waited for; matrix products, arithmetic and copies ran while one was open for 5% of the time, Pallas kernels for 20%

profile of v3, /device:TPU:1, one launch (start us, length us, event | category | flops | bytes accessed | tf_op | source)
XLA Modules:
  0.0 159.7 jit_solution(3266539008363915319)
XLA Ops:
  0.6 0.0 copy-start
  0.6 0.0 copy-start.5
  0.7 0.0 copy-start.6
  0.7 2.2 %collective-permute-start = (f32[1]{0:T(128)}, f32[1]{0:T(128)}, u32[]{:S(2)}, u32[]{:S(2)}) collective-permute-start(f32[1]{0:T(128)} %param.13), channel_id=1, source_target_pairs={{0,1},{1,2},{2,3},{3,4},{4,5},{5,6},{6,7},{7,0},{8,9},{9,10},{10,1... | collective-permute-start | bytes 20 | tf_op jit(solution)/shard_map/ppermute | solution.py:274
  2.9 1.1 slice_bitcast_fusion
  3.9 2.9 %collective-permute-start.2 = (f32[2,256,256]{2,1,0:T(8,128)S(1)}, f32[2,256,256]{2,1,0:T(8,128)S(1)}, u32[]{:S(2)}, u32[]{:S(2)}) collective-permute-start(f32[2,256,256]{2,1,0:T(8,128)S(1)} %slice_bitcast_fusion), channel_id=1, source_target_pairs={{0,7},{1,0},{2,1},{3,2},{4,3},{5,4},{6,5},{7,6},{8,15},{9,8},{10,9... | collective-permute-start | bytes 1572872 | tf_op jit(solution)/shard_map/ppermute | solution.py:274
  6.9 1.4 slice.32
  8.3 0.0 copy-start.2
  8.4 0.1 collective-permute-start.6
  8.5 1.7 %convolution_bitcast_fusion = f32[2,256,256]{1,2,0:T(8,128)S(1)} fusion(f32[256,256,1]{1,0,2:T(8,128)} %constant.21, f32[2,256,256]{2,1,0:T(8,128)S(1)} %copy-done), kind=kOutput, calls=%fused_computation | convolution fusion | flops 402653184 | bytes 1310720 | tf_op jit(solution)/shard_map/ij,cjk,lk->cil/dot_general | solution.py:282
  10.2 0.6 fusion
  11.5 0.0 copy-start.3
  11.5 2.7 %subtract_bitcast_fusion = (f32[1,256,256]{2,1,0:T(8,128)S(1)}, f32[1,256,256]{2,1,0:T(8,128)S(1)}, f32[1,256,256]{2,1,0:T(8,128)S(1)}, f32[1,256,256]{2,1,0:T(8...) fusion(f32[2,256,256]{2,1,0:T(8,128)S(1)} %fusion, ...), kind=kLoop, calls=%fused_computation.11 | loop fusion | flops 917504 | bytes 2883592 | tf_op jit(solution)/shard_map/stack | solution.py:285
  14.3 3.5 %collective-permute-start.1 = (f32[2,256,256]{2,1,0:T(8,128)S(1)}, f32[2,256,256]{2,1,0:T(8,128)S(1)}, u32[]{:S(2)}, u32[]{:S(2)}) collective-permute-start(f32[2,256,256]{2,1,0:T(8,128)S(1)} %slice.25), channel_id=1, source_target_pairs={{0,7},{1,0},{2,1},{3,2},{4,3},{5,4},{6,5},{7,6},{8,15},{9,8},{10,9... | collective-permute-start | bytes 1572872 | tf_op jit(solution)/shard_map/ppermute | solution.py:274
  17.8 0.1 slice.28
  17.9 0.1 collective-permute-start.5
  18.1 5.0 %first_step.6 = (f32[2,2,256,256]{3,2,1,0:T(8,128)S(1)}, f32[2,256,256]{2,1,0:T(8,128)S(1)}, f32[8,128]{1,0:T(8,128)S(1)}) custom-call(f32[2,8,256,256]{3,2,1,0:T(8,128)S(1)} %bitcast.61, f32[2,256,256]{2,1,0:T(8,128)S(1)} %collective-permute-done.2.a_ref, f32[2,256,256]{2,1,0:T(8,128)S(1)} %pad_maximum_fusion.1.q_ref, ...), custom_call_target="tpu_custom_call", output_to_operand_aliasing={{1}: (4, {}), {2}: (5, {})} | custom-call | flops 5000000000 | bytes 800000 | tf_op jit(solution)/shard_map/first_step/pallas_call | solution.py:186
  23.0 3.5 %collective-permute-start.8 = (f32[2,2,256,256]{3,2,1,0:T(8,128)S(1)}, f32[2,2,256,256]{3,2,1,0:T(8,128)S(1)}, u32[]{:S(2)}, u32[]{:S(2)}) collective-permute-start(f32[2,2,256,256]{3,2,1,0:T(8,128)S(1)} %get-tuple-element.49), channel_id=1, source_target_pairs={{0,3},{1,0},{2,5},{3,6},{4,7},{5,4},{6,1},{7,2},{8,11},{9,8},{10,1... | collective-permute-start | bytes 3145736 | tf_op jit(solution)/shard_map/ppermute | solution.py:274
  26.5 1.9 %collective-permute-done.1.a_ref = f32[2,256,256]{2,1,0:T(8,128)S(1)} collective-permute-done((f32[2,256,256]{2,1,0:T(8,128)S(1)}, f32[2,256,256]{2,1,0:T(8,128)S(1)}, u32[]{:S(2)}, u32[]{:S(2)}) %collective-permute-start.1) | collective-permute-done | bytes 524320 | tf_op jit(solution)/shard_map/ppermute | solution.py:274
  28.5 2.3 %first_step.7 = (f32[2,1,256,256]{3,2,1,0:T(8,128)S(1)}, f32[2,256,256]{2,1,0:T(8,128)S(1)}, f32[8,128]{1,0:T(8,128)S(1)}) custom-call(f32[2,8,256,256]{3,2,1,0:T(8,128)S(1)} %bitcast.62, f32[2,256,256]{2,1,0:T(8,128)S(1)} %collective-permute-done.1.a_ref, f32[2,256,256]{2,1,0:T(8,128)S(1)} %pad_maximum_fusion.1.q_ref, ...), custom_call_target="tpu_custom_call", output_to_operand_aliasing={{1}: (4, {}), {2}: (5, {})} | custom-call | flops 30000001024 | bytes 400000 | tf_op jit(solution)/shard_map/first_step/pallas_call | solution.py:186
  30.8 3.4 %collective-permute-done.6.f_ref = f32[2,2,256,256]{3,2,1,0:T(8,128)S(1)} collective-permute-done((f32[2,2,256,256]{3,2,1,0:T(8,128)S(1)}, f32[2,2,256,256]{3,2,1,0:T(8,128)S(1)}, u32[]{:S(2)}, u32[]{:S(2)}) %collective-permute-start.6) | collective-permute-done | bytes 1048608 | tf_op jit(solution)/shard_map/ppermute | solution.py:274
  34.3 5.0 %first_step.8 = (f32[2,2,256,256]{3,2,1,0:T(8,128)S(1)}, f32[2,256,256]{2,1,0:T(8,128)S(1)}, f32[8,128]{1,0:T(8,128)S(1)}) custom-call(f32[2,2,256,256]{3,2,1,0:T(8,128)S(1)} %collective-permute-done.6.f_ref, f32[8,256,256]{2,1,0:T(8,128)S(1)} %bitcast.51, f32[2,256,256]{2,1,0:T(8,128)S(1)} %pad_maximum_fusion.q_ref, ...), custom_call_target="tpu_custom_call", output_to_operand_aliasing={{1}: (4, {}), {2}: (5, {})} | custom-call | flops 3000000000 | bytes 800000 | tf_op jit(solution)/shard_map/first_step/pallas_call | solution.py:186
  39.3 0.1 collective-permute-start.11
  39.4 3.1 %collective-permute-start.3 = (f32[2,1,256,256]{3,2,1,0:T(8,128)S(1)}, f32[2,1,256,256]{3,2,1,0:T(8,128)S(1)}, u32[]{:S(2)}, u32[]{:S(2)}) collective-permute-start(f32[2,1,256,256]{3,2,1,0:T(8,128)S(1)} %get-tuple-element.40), channel_id=1, source_target_pairs={{0,3},{1,0},{2,5},{3,6},{4,7},{5,4},{6,1},{7,2},{8,11},{9,8},{10,1... | collective-permute-start | bytes 1572872 | tf_op jit(solution)/shard_map/ppermute | solution.py:274
  42.5 8.4 %collective-permute-done.8 = f32[2,2,256,256]{3,2,1,0:T(8,128)S(1)} collective-permute-done((f32[2,2,256,256]{3,2,1,0:T(8,128)S(1)}, f32[2,2,256,256]{3,2,1,0:T(8,128)S(1)}, u32[]{:S(2)}, u32[]{:S(2)}) %collective-permute-start.8) | collective-permute-done | bytes 1048608 | tf_op jit(solution)/shard_map/ppermute | solution.py:274
  50.9 3.4 %collective-permute-start.9 = (f32[2,2,256,256]{3,2,1,0:T(8,128)S(1)}, f32[2,2,256,256]{3,2,1,0:T(8,128)S(1)}, u32[]{:S(2)}, u32[]{:S(2)}) collective-permute-start(f32[2,2,256,256]{3,2,1,0:T(8,128)S(1)} %collective-permute-done.8), channel_id=1, source_target_pairs={{3,2},{0,3},{5,4},{6,5},{7,6},{4,7},{1,0},{2,1},{11,10},{8,11},{13... | collective-permute-start | bytes 3145736 | tf_op jit(solution)/shard_map/ppermute | solution.py:274
  54.3 2.4 %first_step.9 = (f32[2,1,256,256]{3,2,1,0:T(8,128)S(1)}, f32[2,256,256]{2,1,0:T(8,128)S(1)}, f32[8,128]{1,0:T(8,128)S(1)}) custom-call(f32[2,8,256,256]{3,2,1,0:T(8,128)S(1)} %bitcast.63, f32[2,256,256]{2,1,0:T(8,128)S(1)} %collective-permute-done.1.a_ref, f32[2,256,256]{2,1,0:T(8,128)S(1)} %pad_maximum_fusion.1.q_ref, ...), custom_call_target="tpu_custom_call", output_to_operand_aliasing={{1}: (4, {}), {2}: (5, {})} | custom-call | flops 1000000000 | bytes 400000 | tf_op jit(solution)/shard_map/first_step/pallas_call | solution.py:186
  56.7 0.3 collective-permute-start.10
  57.1 2.4 %first_step.10 = (f32[2,1,256,256]{3,2,1,0:T(8,128)S(1)}, f32[2,256,256]{2,1,0:T(8,128)S(1)}, f32[8,128]{1,0:T(8,128)S(1)}) custom-call(f32[2,2,256,256]{3,2,1,0:T(8,128)S(1)} %collective-permute-done.5.f_ref, f32[8,256,256]{2,1,0:T(8,128)S(1)} %bitcast.52, f32[2,256,256]{2,1,0:T(8,128)S(1)} %pad_maximum_fusion.q_ref, ...), custom_call_target="tpu_custom_call", output_to_operand_aliasing={{1}: (4, {}), {2}: (5, {})} | custom-call | flops 100000000 | bytes 400000 | tf_op jit(solution)/shard_map/first_step/pallas_call | solution.py:186
  59.4 0.5 collective-permute-start.7
  59.9 2.4 %first_step.11 = (f32[2,1,256,256]{3,2,1,0:T(8,128)S(1)}, f32[2,256,256]{2,1,0:T(8,128)S(1)}, f32[8,128]{1,0:T(8,128)S(1)}) custom-call(f32[2,2,256,256]{3,2,1,0:T(8,128)S(1)} %collective-permute-done.5.f_ref, f32[8,256,256]{2,1,0:T(8,128)S(1)} %bitcast.53, f32[2,256,256]{2,1,0:T(8,128)S(1)} %pad_maximum_fusion.q_ref, ...), custom_call_target="tpu_custom_call", output_to_operand_aliasing={{1}: (4, {}), {2}: (5, {})} | custom-call | flops 5000000000 | bytes 400000 | tf_op jit(solution)/shard_map/first_step/pallas_call | solution.py:186
  62.3 2.5 %collective-permute-start.12 = (f32[2,1,256,256]{3,2,1,0:T(8,128)S(1)}, f32[2,1,256,256]{3,2,1,0:T(8,128)S(1)}, u32[]{:S(2)}, u32[]{:S(2)}) collective-permute-start(f32[2,1,256,256]{3,2,1,0:T(8,128)S(1)} %get-tuple-element.66), channel_id=1, source_target_pairs={{0,1},{1,2},{2,3},{3,4},{4,5},{5,6},{6,7},{7,0},{8,9},{9,10},{10,1... | collective-permute-start | bytes 1572872 | tf_op jit(solution)/shard_map/ppermute | solution.py:274
  64.8 15.7 %collective-permute-done.11.s_ref = f32[2,2,256,256]{3,2,1,0:T(8,128)S(1)} collective-permute-done((f32[2,2,256,256]{3,2,1,0:T(8,128)S(1)}, f32[2,2,256,256]{3,2,1,0:T(8,128)S(1)}, u32[]{:S(2)}, u32[]{:S(2)}) %collective-permute-start.11) | collective-permute-done | bytes 1048608 | tf_op jit(solution)/shard_map/ppermute | solution.py:274
  80.5 6.9 %collective-permute-start.4 = (f32[2,1,256,256]{3,2,1,0:T(8,128)S(1)}, f32[2,1,256,256]{3,2,1,0:T(8,128)S(1)}, u32[]{:S(2)}, u32[]{:S(2)}) collective-permute-start(f32[2,1,256,256]{3,2,1,0:T(8,128)S(1)} %collective-permute-done.3), channel_id=1, source_target_pairs={{3,2},{0,3},{5,4},{6,5},{7,6},{4,7},{1,0},{2,1},{11,10},{8,11},{13... | collective-permute-start | bytes 1572872 | tf_op jit(solution)/shard_map/ppermute | solution.py:274
  87.4 4.1 %second_step.5 = (f32[2,8,256,256]{3,2,1,0:T(8,128)}, f32[2,256,256]{2,1,0:T(8,128)S(1)}, f32[8,128]{1,0:T(8,128)S(1)}) custom-call(f32[2,2,256,256]{3,2,1,0:T(8,128)S(1)} %collective-permute-done.11.s_ref, f32[8,256,256]{2,1,0:T(8,128)S(1)} %bitcast.54, f32[2,256,256]{2,1,0:T(8,128)S(1)} %pad_maximum_fusion.q_ref, ...), custom_call_target="tpu_custom_call", output_to_operand_aliasing={{1}: (4, {}), {2}: (5, {})} | custom-call | flops 3000000000 | bytes 800000 | tf_op jit(solution)/shard_map/second_step/pallas_call | solution.py:186
  91.6 2.4 %second_step.6 = (f32[2,8,256,256]{3,2,1,0:T(8,128)}, f32[2,256,256]{2,1,0:T(8,128)S(1)}, f32[8,128]{1,0:T(8,128)S(1)}) custom-call(f32[2,1,256,256]{3,2,1,0:T(8,128)S(1)} %collective-permute-done.10.s_ref, f32[8,256,256]{2,1,0:T(8,128)S(1)} %bitcast.55, ...), custom_call_target="tpu_custom_call", output_to_operand_aliasing={{1}: (4, {}), {2}: (5, {}), {0}: (6, {})} | custom-call | flops 3000000000 | bytes 400000 | tf_op jit(solution)/shard_map/second_step/pallas_call | solution.py:186
  94.0 4.2 %second_step.7 = (f32[2,8,256,256]{3,2,1,0:T(8,128)}, f32[2,256,256]{2,1,0:T(8,128)S(1)}, f32[8,128]{1,0:T(8,128)S(1)}) custom-call(f32[2,2,256,256]{3,2,1,0:T(8,128)S(1)} %collective-permute-done.9.s_ref, f32[8,256,256]{2,1,0:T(8,128)S(1)} %bitcast.56, ...), custom_call_target="tpu_custom_call", output_to_operand_aliasing={{1}: (4, {}), {2}: (5, {}), {0}: (6, {})} | custom-call | flops 3000000000 | bytes 800000 | tf_op jit(solution)/shard_map/second_step/pallas_call | solution.py:186
  98.1 3.5 %collective-permute-done.7.s_ref = f32[2,1,256,256]{3,2,1,0:T(8,128)S(1)} collective-permute-done((f32[2,1,256,256]{3,2,1,0:T(8,128)S(1)}, f32[2,1,256,256]{3,2,1,0:T(8,128)S(1)}, u32[]{:S(2)}, u32[]{:S(2)}) %collective-permute-start.7) | collective-permute-done | bytes 524320 | tf_op jit(solution)/shard_map/ppermute | solution.py:274
  101.7 2.4 %second_step.8 = (f32[2,8,256,256]{3,2,1,0:T(8,128)}, f32[2,256,256]{2,1,0:T(8,128)S(1)}, f32[8,128]{1,0:T(8,128)S(1)}) custom-call(f32[2,1,256,256]{3,2,1,0:T(8,128)S(1)} %collective-permute-done.7.s_ref, f32[8,256,256]{2,1,0:T(8,128)S(1)} %bitcast.57, ...), custom_call_target="tpu_custom_call", output_to_operand_aliasing={{1}: (4, {}), {2}: (5, {}), {0}: (6, {})} | custom-call | flops 10000000000 | bytes 400000 | tf_op jit(solution)/shard_map/second_step/pallas_call | solution.py:186
  104.1 3.0 %collective-permute-done.4.s_ref = f32[2,1,256,256]{3,2,1,0:T(8,128)S(1)} collective-permute-done((f32[2,1,256,256]{3,2,1,0:T(8,128)S(1)}, f32[2,1,256,256]{3,2,1,0:T(8,128)S(1)}, u32[]{:S(2)}, u32[]{:S(2)}) %collective-permute-start.4) | collective-permute-done | bytes 524320 | tf_op jit(solution)/shard_map/ppermute | solution.py:274
  107.1 5.8 %collective-permute-done.12.other_ref = f32[2,1,256,256]{3,2,1,0:T(8,128)S(1)} collective-permute-done((f32[2,1,256,256]{3,2,1,0:T(8,128)S(1)}, f32[2,1,256,256]{3,2,1,0:T(8,128)S(1)}, u32[]{:S(2)}, u32[]{:S(2)}) %collective-permute-start.12) | collective-permute-done | bytes 524320 | tf_op jit(solution)/shard_map/ppermute | solution.py:274
  112.9 4.1 %second_step.9 = (f32[2,8,256,256]{3,2,1,0:T(8,128)}, f32[2,256,256]{2,1,0:T(8,128)S(1)}, f32[8,128]{1,0:T(8,128)S(1)}) custom-call(f32[2,1,256,256]{3,2,1,0:T(8,128)S(1)} %collective-permute-done.4.s_ref, f32[8,256,256]{2,1,0:T(8,128)S(1)} %bitcast.58, ...), custom_call_target="tpu_custom_call", output_to_operand_aliasing={{1}: (4, {}), {2}: (6, {}), {0}: (7, {})} | custom-call | flops 1000000000 | bytes 800000 | tf_op jit(solution)/shard_map/second_step/pallas_call | solution.py:206
  117.0 1.0 finish.1
  118.0 22.6 %all_to_all.11 = f32[128,8,128]{2,1,0:T(8,128)S(1)} all-to-all(f32[128,8,128]{2,1,0:T(8,128)S(1)} %bitcast.64), channel_id=1, replica_groups=mesh['tile'=16,'plane'=8] {'tile','plane'}, dimensions={0} | all-to-all | bytes 1048576 | tf_op jit(solution)/shard_map/all_to_all | solution.py:254
  140.5 0.1 reduce_sum.9
  140.7 17.8 %all_to_all.10 = f32[128,8,128]{2,1,0:T(8,128)S(1)} all-to-all(f32[128,8,128]{2,1,0:T(8,128)S(1)} %broadcast_in_dim.14), channel_id=1, replica_groups=mesh['tile'=16,'plane'=8] {'tile','plane'}, dimensions={0} | all-to-all | bytes 1048576 | tf_op jit(solution)/shard_map/all_to_all | solution.py:256
  158.5 0.2 copy.40
  158.7 1.0 copy.42
  (22 shorter events, 0.3 us)
Async XLA Ops:
  0.6 7.8 %copy-start = (f32[2,256,256]{2,1,0:T(8,128)S(1)}, f32[2,256,256]{2,1,0:T(8,128)}, u32[]{:S(2)}) copy-start(f32[2,256,256]{2,1,0:T(8,128)} %param.12) | copy-start | bytes 1572868
  0.6 9.5 %copy-start.5 = (f32[256,256,1]{1,0,2:T(8,128)S(1)}, f32[256,256,1]{1,0,2:T(8,128)}, u32[]{:S(2)}) copy-start(f32[256,256,1]{1,0,2:T(8,128)} %constant.21) | copy-start | bytes 786436
  0.7 10.8 %copy-start.6 = (f32[256,256]{1,0:T(8,128)S(1)}, f32[256,256]{1,0:T(8,128)}, u32[]{:S(2)}) copy-start(f32[256,256]{1,0:T(8,128)} %constant.16.clone) | copy-start | bytes 786436
  0.7 10.8 %collective-permute-start = (f32[1]{0:T(128)}, f32[1]{0:T(128)}, u32[]{:S(2)}, u32[]{:S(2)}) collective-permute-start(f32[1]{0:T(128)} %param.13), channel_id=1, source_target_pairs={{0,1},{1,2},{2,3},{3,4},{4,5},{5,6},{6,7},{7,0},{8,9},{9,10},{10,1... | collective-permute-start | bytes 20 | tf_op jit(solution)/shard_map/ppermute | solution.py:274
  3.9 14.1 %collective-permute-start.2 = (f32[2,256,256]{2,1,0:T(8,128)S(1)}, f32[2,256,256]{2,1,0:T(8,128)S(1)}, u32[]{:S(2)}, u32[]{:S(2)}) collective-permute-start(f32[2,256,256]{2,1,0:T(8,128)S(1)} %slice_bitcast_fusion), channel_id=1, source_target_pairs={{0,7},{1,0},{2,1},{3,2},{4,3},{5,4},{6,5},{7,6},{8,15},{9,8},{10,9... | collective-permute-start | bytes 1572872 | tf_op jit(solution)/shard_map/ppermute | solution.py:274
  6.9 7.4 %copy-start.1 = (f32[1,8,256,256]{3,2,1,0:T(8,128)S(1)}, f32[1,8,256,256]{3,2,1,0:T(8,128)}, u32[]{:S(2)}) copy-start(f32[1,8,256,256]{3,2,1,0:T(8,128)} %param.11) | copy-start | bytes 6291460
  8.3 9.4 %copy-start.2 = (f32[2,1,8,256,256]{4,3,2,1,0:T(8,128)S(1)}, f32[2,1,8,256,256]{4,3,2,1,0:T(8,128)}, u32[]{:S(2)}) copy-start(f32[2,1,8,256,256]{4,3,2,1,0:T(8,128)} %param.10) | copy-start | bytes 12582916
  8.4 25.9 %collective-permute-start.6 = (f32[2,2,256,256]{3,2,1,0:T(8,128)S(1)}, f32[2,2,256,256]{3,2,1,0:T(8,128)S(1)}, u32[]{:S(2)}, u32[]{:S(2)}) collective-permute-start(f32[2,2,256,256]{3,2,1,0:T(8,128)S(1)} %slice.32), channel_id=1, source_target_pairs={{0,1},{1,2},{2,3},{3,4},{4,5},{5,6},{6,7},{7,0},{8,9},{9,10},{10,1... | collective-permute-start | bytes 3145736 | tf_op jit(solution)/shard_map/ppermute | solution.py:274
  11.5 6.6 %copy-start.3 = (bf16[2,4,256,256]{3,2,1,0:T(8,128)(2,1)S(1)}, bf16[2,4,256,256]{3,2,1,0:T(8,128)(2,1)}, u32[]{:S(2)}) copy-start(bf16[2,4,256,256]{3,2,1,0:T(8,128)(2,1)} %constant.4.clone.tables) | copy-start | bytes 3145732
  14.3 14.2 %collective-permute-start.1 = (f32[2,256,256]{2,1,0:T(8,128)S(1)}, f32[2,256,256]{2,1,0:T(8,128)S(1)}, u32[]{:S(2)}, u32[]{:S(2)}) collective-permute-start(f32[2,256,256]{2,1,0:T(8,128)S(1)} %slice.25), channel_id=1, source_target_pairs={{0,7},{1,0},{2,1},{3,2},{4,3},{5,4},{6,5},{7,6},{8,15},{9,8},{10,9... | collective-permute-start | bytes 1572872 | tf_op jit(solution)/shard_map/ppermute | solution.py:274
  17.9 39.2 %collective-permute-start.5 = (f32[2,2,256,256]{3,2,1,0:T(8,128)S(1)}, f32[2,2,256,256]{3,2,1,0:T(8,128)S(1)}, u32[]{:S(2)}, u32[]{:S(2)}) collective-permute-start(f32[2,2,256,256]{3,2,1,0:T(8,128)S(1)} %slice.28), channel_id=1, source_target_pairs={{0,1},{1,2},{2,3},{3,4},{4,5},{5,6},{6,7},{7,0},{8,9},{9,10},{10,1... | collective-permute-start | bytes 3145736 | tf_op jit(solution)/shard_map/ppermute | solution.py:274
  23.0 27.9 %collective-permute-start.8 = (f32[2,2,256,256]{3,2,1,0:T(8,128)S(1)}, f32[2,2,256,256]{3,2,1,0:T(8,128)S(1)}, u32[]{:S(2)}, u32[]{:S(2)}) collective-permute-start(f32[2,2,256,256]{3,2,1,0:T(8,128)S(1)} %get-tuple-element.49), channel_id=1, source_target_pairs={{0,3},{1,0},{2,5},{3,6},{4,7},{5,4},{6,1},{7,2},{8,11},{9,8},{10,1... | collective-permute-start | bytes 3145736 | tf_op jit(solution)/shard_map/ppermute | solution.py:274
  39.3 41.2 %collective-permute-start.11 = (f32[2,2,256,256]{3,2,1,0:T(8,128)S(1)}, f32[2,2,256,256]{3,2,1,0:T(8,128)S(1)}, u32[]{:S(2)}, u32[]{:S(2)}) collective-permute-start(f32[2,2,256,256]{3,2,1,0:T(8,128)S(1)} %get-tuple-element.51), channel_id=1, source_target_pairs={{0,1},{1,2},{2,3},{3,4},{4,5},{5,6},{6,7},{7,0},{8,9},{9,10},{10,1... | collective-permute-start | bytes 3145736 | tf_op jit(solution)/shard_map/ppermute | solution.py:274
  39.4 22.9 %collective-permute-start.3 = (f32[2,1,256,256]{3,2,1,0:T(8,128)S(1)}, f32[2,1,256,256]{3,2,1,0:T(8,128)S(1)}, u32[]{:S(2)}, u32[]{:S(2)}) collective-permute-start(f32[2,1,256,256]{3,2,1,0:T(8,128)S(1)} %get-tuple-element.40), channel_id=1, source_target_pairs={{0,3},{1,0},{2,5},{3,6},{4,7},{5,4},{6,1},{7,2},{8,11},{9,8},{10,1... | collective-permute-start | bytes 1572872 | tf_op jit(solution)/shard_map/ppermute | solution.py:274
  50.9 43.1 %collective-permute-start.9 = (f32[2,2,256,256]{3,2,1,0:T(8,128)S(1)}, f32[2,2,256,256]{3,2,1,0:T(8,128)S(1)}, u32[]{:S(2)}, u32[]{:S(2)}) collective-permute-start(f32[2,2,256,256]{3,2,1,0:T(8,128)S(1)} %collective-permute-done.8), channel_id=1, source_target_pairs={{3,2},{0,3},{5,4},{6,5},{7,6},{4,7},{1,0},{2,1},{11,10},{8,11},{13... | collective-permute-start | bytes 3145736 | tf_op jit(solution)/shard_map/ppermute | solution.py:274
  56.7 34.8 %collective-permute-start.10 = (f32[2,1,256,256]{3,2,1,0:T(8,128)S(1)}, f32[2,1,256,256]{3,2,1,0:T(8,128)S(1)}, u32[]{:S(2)}, u32[]{:S(2)}) collective-permute-start(f32[2,1,256,256]{3,2,1,0:T(8,128)S(1)} %get-tuple-element.50), channel_id=1, source_target_pairs={{0,2},{1,3},{2,4},{3,5},{4,6},{5,7},{6,0},{7,1},{8,10},{9,11},{10,... | collective-permute-start | bytes 1572872 | tf_op jit(solution)/shard_map/ppermute | solution.py:274
  59.4 42.2 %collective-permute-start.7 = (f32[2,1,256,256]{3,2,1,0:T(8,128)S(1)}, f32[2,1,256,256]{3,2,1,0:T(8,128)S(1)}, u32[]{:S(2)}, u32[]{:S(2)}) collective-permute-start(f32[2,1,256,256]{3,2,1,0:T(8,128)S(1)} %get-tuple-element.48), channel_id=1, source_target_pairs={{0,1},{1,2},{2,3},{3,4},{4,5},{5,6},{6,7},{7,0},{8,9},{9,10},{10,1... | collective-permute-start | bytes 1572872 | tf_op jit(solution)/shard_map/ppermute | solution.py:274
  62.3 50.6 %collective-permute-start.12 = (f32[2,1,256,256]{3,2,1,0:T(8,128)S(1)}, f32[2,1,256,256]{3,2,1,0:T(8,128)S(1)}, u32[]{:S(2)}, u32[]{:S(2)}) collective-permute-start(f32[2,1,256,256]{3,2,1,0:T(8,128)S(1)} %get-tuple-element.66), channel_id=1, source_target_pairs={{0,1},{1,2},{2,3},{3,4},{4,5},{5,6},{6,7},{7,0},{8,9},{9,10},{10,1... | collective-permute-start | bytes 1572872 | tf_op jit(solution)/shard_map/ppermute | solution.py:274
  80.5 26.6 %collective-permute-start.4 = (f32[2,1,256,256]{3,2,1,0:T(8,128)S(1)}, f32[2,1,256,256]{3,2,1,0:T(8,128)S(1)}, u32[]{:S(2)}, u32[]{:S(2)}) collective-permute-start(f32[2,1,256,256]{3,2,1,0:T(8,128)S(1)} %collective-permute-done.3), channel_id=1, source_target_pairs={{3,2},{0,3},{5,4},{6,5},{7,6},{4,7},{1,0},{2,1},{11,10},{8,11},{13... | collective-permute-start | bytes 1572872 | tf_op jit(solution)/shard_map/ppermute | solution.py:274
  112.9 4.1 %copy-start.4 = (bf16[2,256,256]{2,1,0:T(8,128)(2,1)S(1)}, bf16[2,256,256]{2,1,0:T(8,128)(2,1)}, u32[]{:S(2)}) copy-start(bf16[2,256,256]{2,1,0:T(8,128)(2,1)} %constant.17.clone.mix) | copy-start | bytes 786436

commit v4 on v3

--- a/solution.py
+++ b/solution.py
@@ -304,7 +304,7 @@
         out, grads["before"], token = step_call(
             second_kernel, x, 0, amps, at, filters["before"], tables, grads["before"], token, tiles, out, at, count, (), weight, "second_step")
 
-    weights = [5, 30, 3, 1, 0.1, 5, 3, 10]
+    weights = [5, 20, 0.1, 20, 3, 0.1, 1, 20]
     s_45 = sent(first("here", fields, 4, amps_45, 0, 2, weights[0]), back)
     s_6 = sent(first("here", fields, 6, amps_67, 0, 1, weights[1]), back)
     s_01 = sent(first("before", fields_01, 0, amps, 0, 2, weights[2]), ahead)

time: 160 us -> 160 us (level)
  transfers between devices with their start and end apart: 13 -> 13, of which waited for: 7 -> 6; matrix products, arithmetic and copies ran while one was open for 5% -> 5% of each run, Pallas kernels for 20% -> 20%
where the time goes in v4:
time: 160 us
  waiting for transfers between devices  41 us (26%)
  blocking collectives  40.4 us (25%)
  Pallas kernels  37.7 us (24%)
  starting transfers between devices  29.9 us (19%)
  local copies, waits for them, and re-layouts  3.98 us (2%)
  other arithmetic  2.91 us (2%)
  matrix products  2.34 us (1%)
    ppermute x13, waiting for transfers between devices, sent(): return lax.ppermute(value, 'plane', pairs)  41 us
    pallas_call x10, Pallas kernels, step_call(): pl.pallas_call(kernel, grid=(tiles,), in_specs=[tile_spec(x.shape, x_at),...  32.6 us
    ppermute x13, starting transfers between devices, sent(): return lax.ppermute(value, 'plane', pairs)  29.9 us
    all_to_all x1, blocking collectives, summed(): mine = lax.all_to_all(mine, AXES, 0, 0, tiled=True).sum(0)  22.6 us
    all_to_all x1, blocking collectives, summed(): lax.all_to_all(mine, AXES, 0, 0, tiled=True).reshape(2, 2, WIDTH, HALF)  17.8 us
    pallas_call x1, Pallas kernels, last_step(): pl.pallas_call(last_kernel, grid=(2,), in_specs=[whole(x.shape), tile_spe...  4.1 us
  transfers between devices with their start and end apart: 13, of which 6 were waited for; matrix products, arithmetic and copies ran while one was open for 5% of the time, Pallas kernels for 20%

profile of v4, /device:TPU:1, one launch (start us, length us, event | category | flops | bytes accessed | tf_op | source)
XLA Modules:
  0.0 159.7 jit_solution(3722863354185412480)
XLA Ops:
  0.6 0.0 copy-start
  0.6 0.0 copy-start.5
  0.7 0.0 copy-start.6
  0.7 2.2 %collective-permute-start = (f32[1]{0:T(128)}, f32[1]{0:T(128)}, u32[]{:S(2)}, u32[]{:S(2)}) collective-permute-start(f32[1]{0:T(128)} %param.13), channel_id=1, source_target_pairs={{0,1},{1,2},{2,3},{3,4},{4,5},{5,6},{6,7},{7,0},{8,9},{9,10},{10,1... | collective-permute-start | bytes 20 | tf_op jit(solution)/shard_map/ppermute | solution.py:274
  2.9 1.1 slice_bitcast_fusion
  3.9 2.9 %collective-permute-start.2 = (f32[2,256,256]{2,1,0:T(8,128)S(1)}, f32[2,256,256]{2,1,0:T(8,128)S(1)}, u32[]{:S(2)}, u32[]{:S(2)}) collective-permute-start(f32[2,256,256]{2,1,0:T(8,128)S(1)} %slice_bitcast_fusion), channel_id=1, source_target_pairs={{0,7},{1,0},{2,1},{3,2},{4,3},{5,4},{6,5},{7,6},{8,15},{9,8},{10,9... | collective-permute-start | bytes 1572872 | tf_op jit(solution)/shard_map/ppermute | solution.py:274
  6.9 1.4 slice.32
  8.3 0.0 copy-start.3
  8.4 0.1 collective-permute-start.6
  8.4 1.7 %convolution_bitcast_fusion = f32[2,256,256]{1,2,0:T(8,128)S(1)} fusion(f32[256,256,1]{1,0,2:T(8,128)} %constant.21, f32[2,256,256]{2,1,0:T(8,128)S(1)} %copy-done), kind=kOutput, calls=%fused_computation | convolution fusion | flops 402653184 | bytes 1310720 | tf_op jit(solution)/shard_map/ij,cjk,lk->cil/dot_general | solution.py:282
  10.2 0.6 fusion
  11.5 0.0 collective-permute-done
  11.5 0.0 copy-start.2
  11.5 2.7 %subtract_bitcast_fusion = (f32[1,256,256]{2,1,0:T(8,128)S(1)}, f32[1,256,256]{2,1,0:T(8,128)S(1)}, f32[1,256,256]{2,1,0:T(8,128)S(1)}, f32[1,256,256]{2,1,0:T(8...) fusion(f32[2,256,256]{2,1,0:T(8,128)S(1)} %fusion, ...), kind=kLoop, calls=%fused_computation.11 | loop fusion | flops 917504 | bytes 2883592 | tf_op jit(solution)/shard_map/stack | solution.py:285
  14.3 3.5 %collective-permute-start.1 = (f32[2,256,256]{2,1,0:T(8,128)S(1)}, f32[2,256,256]{2,1,0:T(8,128)S(1)}, u32[]{:S(2)}, u32[]{:S(2)}) collective-permute-start(f32[2,256,256]{2,1,0:T(8,128)S(1)} %slice.25), channel_id=1, source_target_pairs={{0,7},{1,0},{2,1},{3,2},{4,3},{5,4},{6,5},{7,6},{8,15},{9,8},{10,9... | collective-permute-start | bytes 1572872 | tf_op jit(solution)/shard_map/ppermute | solution.py:274
  17.8 0.1 slice.28
  17.9 0.1 collective-permute-start.5
  18.1 5.0 %first_step.6 = (f32[2,2,256,256]{3,2,1,0:T(8,128)S(1)}, f32[2,256,256]{2,1,0:T(8,128)S(1)}, f32[8,128]{1,0:T(8,128)S(1)}) custom-call(f32[2,8,256,256]{3,2,1,0:T(8,128)S(1)} %bitcast.62, f32[2,256,256]{2,1,0:T(8,128)S(1)} %collective-permute-done.2.a_ref, f32[2,256,256]{2,1,0:T(8,128)S(1)} %pad_maximum_fusion.1.q_ref, ...), custom_call_target="tpu_custom_call", output_to_operand_aliasing={{1}: (4, {}), {2}: (5, {})} | custom-call | flops 5000000000 | bytes 800000 | tf_op jit(solution)/shard_map/first_step/pallas_call | solution.py:186
  23.1 3.5 %collective-permute-start.8 = (f32[2,2,256,256]{3,2,1,0:T(8,128)S(1)}, f32[2,2,256,256]{3,2,1,0:T(8,128)S(1)}, u32[]{:S(2)}, u32[]{:S(2)}) collective-permute-start(f32[2,2,256,256]{3,2,1,0:T(8,128)S(1)} %get-tuple-element.49), channel_id=1, source_target_pairs={{0,3},{1,0},{2,5},{3,6},{4,7},{5,4},{6,1},{7,2},{8,11},{9,8},{10,1... | collective-permute-start | bytes 3145736 | tf_op jit(solution)/shard_map/ppermute | solution.py:274
  26.5 1.9 %collective-permute-done.1.a_ref = f32[2,256,256]{2,1,0:T(8,128)S(1)} collective-permute-done((f32[2,256,256]{2,1,0:T(8,128)S(1)}, f32[2,256,256]{2,1,0:T(8,128)S(1)}, u32[]{:S(2)}, u32[]{:S(2)}) %collective-permute-start.1) | collective-permute-done | bytes 524320 | tf_op jit(solution)/shard_map/ppermute | solution.py:274
  28.5 2.4 %first_step.7 = (f32[2,1,256,256]{3,2,1,0:T(8,128)S(1)}, f32[2,256,256]{2,1,0:T(8,128)S(1)}, f32[8,128]{1,0:T(8,128)S(1)}) custom-call(f32[2,8,256,256]{3,2,1,0:T(8,128)S(1)} %bitcast.63, f32[2,256,256]{2,1,0:T(8,128)S(1)} %collective-permute-done.1.a_ref, f32[2,256,256]{2,1,0:T(8,128)S(1)} %pad_maximum_fusion.1.q_ref, ...), custom_call_target="tpu_custom_call", output_to_operand_aliasing={{1}: (4, {}), {2}: (5, {})} | custom-call | flops 20000000000 | bytes 400000 | tf_op jit(solution)/shard_map/first_step/pallas_call | solution.py:186
  30.8 3.9 %collective-permute-start.3 = (f32[2,1,256,256]{3,2,1,0:T(8,128)S(1)}, f32[2,1,256,256]{3,2,1,0:T(8,128)S(1)}, u32[]{:S(2)}, u32[]{:S(2)}) collective-permute-start(f32[2,1,256,256]{3,2,1,0:T(8,128)S(1)} %get-tuple-element.40), channel_id=1, source_target_pairs={{0,3},{1,0},{2,5},{3,6},{4,7},{5,4},{6,1},{7,2},{8,11},{9,8},{10,1... | collective-permute-start | bytes 1572872 | tf_op jit(solution)/shard_map/ppermute | solution.py:274
  34.8 5.0 %first_step.8 = (f32[2,2,256,256]{3,2,1,0:T(8,128)S(1)}, f32[2,256,256]{2,1,0:T(8,128)S(1)}, f32[8,128]{1,0:T(8,128)S(1)}) custom-call(f32[2,2,256,256]{3,2,1,0:T(8,128)S(1)} %collective-permute-done.6.f_ref, f32[8,256,256]{2,1,0:T(8,128)S(1)} %bitcast.51, f32[2,256,256]{2,1,0:T(8,128)S(1)} %pad_maximum_fusion.q_ref, ...), custom_call_target="tpu_custom_call", output_to_operand_aliasing={{1}: (4, {}), {2}: (5, {})} | custom-call | flops 100000000 | bytes 800000 | tf_op jit(solution)/shard_map/first_step/pallas_call | solution.py:186
  39.8 0.1 collective-permute-start.11
  39.9 11.0 %collective-permute-done.8 = f32[2,2,256,256]{3,2,1,0:T(8,128)S(1)} collective-permute-done((f32[2,2,256,256]{3,2,1,0:T(8,128)S(1)}, f32[2,2,256,256]{3,2,1,0:T(8,128)S(1)}, u32[]{:S(2)}, u32[]{:S(2)}) %collective-permute-start.8) | collective-permute-done | bytes 1048608 | tf_op jit(solution)/shard_map/ppermute | solution.py:274
  50.9 3.4 %collective-permute-start.9 = (f32[2,2,256,256]{3,2,1,0:T(8,128)S(1)}, f32[2,2,256,256]{3,2,1,0:T(8,128)S(1)}, u32[]{:S(2)}, u32[]{:S(2)}) collective-permute-start(f32[2,2,256,256]{3,2,1,0:T(8,128)S(1)} %collective-permute-done.8), channel_id=1, source_target_pairs={{3,2},{0,3},{5,4},{6,5},{7,6},{4,7},{1,0},{2,1},{11,10},{8,11},{13... | collective-permute-start | bytes 3145736 | tf_op jit(solution)/shard_map/ppermute | solution.py:274
  54.3 2.4 %first_step.9 = (f32[2,1,256,256]{3,2,1,0:T(8,128)S(1)}, f32[2,256,256]{2,1,0:T(8,128)S(1)}, f32[8,128]{1,0:T(8,128)S(1)}) custom-call(f32[2,8,256,256]{3,2,1,0:T(8,128)S(1)} %bitcast.64, f32[2,256,256]{2,1,0:T(8,128)S(1)} %collective-permute-done.1.a_ref, f32[2,256,256]{2,1,0:T(8,128)S(1)} %pad_maximum_fusion.1.q_ref, ...), custom_call_target="tpu_custom_call", output_to_operand_aliasing={{1}: (4, {}), {2}: (5, {})} | custom-call | flops 20000000000 | bytes 400000 | tf_op jit(solution)/shard_map/first_step/pallas_call | solution.py:186
  56.7 0.4 collective-permute-start.10
  57.1 2.4 %first_step.10 = (f32[2,1,256,256]{3,2,1,0:T(8,128)S(1)}, f32[2,256,256]{2,1,0:T(8,128)S(1)}, f32[8,128]{1,0:T(8,128)S(1)}) custom-call(f32[2,2,256,256]{3,2,1,0:T(8,128)S(1)} %collective-permute-done.5.f_ref, f32[8,256,256]{2,1,0:T(8,128)S(1)} %bitcast.52, f32[2,256,256]{2,1,0:T(8,128)S(1)} %pad_maximum_fusion.q_ref, ...), custom_call_target="tpu_custom_call", output_to_operand_aliasing={{1}: (4, {}), {2}: (5, {})} | custom-call | flops 3000000000 | bytes 400000 | tf_op jit(solution)/shard_map/first_step/pallas_call | solution.py:186
  59.5 0.5 collective-permute-start.7
  59.9 2.4 %first_step.11 = (f32[2,1,256,256]{3,2,1,0:T(8,128)S(1)}, f32[2,256,256]{2,1,0:T(8,128)S(1)}, f32[8,128]{1,0:T(8,128)S(1)}) custom-call(f32[2,2,256,256]{3,2,1,0:T(8,128)S(1)} %collective-permute-done.5.f_ref, f32[8,256,256]{2,1,0:T(8,128)S(1)} %bitcast.53, f32[2,256,256]{2,1,0:T(8,128)S(1)} %pad_maximum_fusion.q_ref, ...), custom_call_target="tpu_custom_call", output_to_operand_aliasing={{1}: (4, {}), {2}: (5, {})} | custom-call | flops 100000000 | bytes 400000 | tf_op jit(solution)/shard_map/first_step/pallas_call | solution.py:186
  62.3 2.5 %collective-permute-start.12 = (f32[2,1,256,256]{3,2,1,0:T(8,128)S(1)}, f32[2,1,256,256]{3,2,1,0:T(8,128)S(1)}, u32[]{:S(2)}, u32[]{:S(2)}) collective-permute-start(f32[2,1,256,256]{3,2,1,0:T(8,128)S(1)} %get-tuple-element.66), channel_id=1, source_target_pairs={{0,1},{1,2},{2,3},{3,4},{4,5},{5,6},{6,7},{7,0},{8,9},{9,10},{10,1... | collective-permute-start | bytes 1572872 | tf_op jit(solution)/shard_map/ppermute | solution.py:274
  64.8 15.7 %collective-permute-done.11.s_ref = f32[2,2,256,256]{3,2,1,0:T(8,128)S(1)} collective-permute-done((f32[2,2,256,256]{3,2,1,0:T(8,128)S(1)}, f32[2,2,256,256]{3,2,1,0:T(8,128)S(1)}, u32[]{:S(2)}, u32[]{:S(2)}) %collective-permute-start.11) | collective-permute-done | bytes 1048608 | tf_op jit(solution)/shard_map/ppermute | solution.py:274
  80.5 6.9 %collective-permute-start.4 = (f32[2,1,256,256]{3,2,1,0:T(8,128)S(1)}, f32[2,1,256,256]{3,2,1,0:T(8,128)S(1)}, u32[]{:S(2)}, u32[]{:S(2)}) collective-permute-start(f32[2,1,256,256]{3,2,1,0:T(8,128)S(1)} %collective-permute-done.3), channel_id=1, source_target_pairs={{3,2},{0,3},{5,4},{6,5},{7,6},{4,7},{1,0},{2,1},{11,10},{8,11},{13... | collective-permute-start | bytes 1572872 | tf_op jit(solution)/shard_map/ppermute | solution.py:274
  87.4 4.2 %second_step.5 = (f32[2,8,256,256]{3,2,1,0:T(8,128)}, f32[2,256,256]{2,1,0:T(8,128)S(1)}, f32[8,128]{1,0:T(8,128)S(1)}) custom-call(f32[2,2,256,256]{3,2,1,0:T(8,128)S(1)} %collective-permute-done.11.s_ref, f32[8,256,256]{2,1,0:T(8,128)S(1)} %bitcast.54, f32[2,256,256]{2,1,0:T(8,128)S(1)} %pad_maximum_fusion.q_ref, ...), custom_call_target="tpu_custom_call", output_to_operand_aliasing={{1}: (4, {}), {2}: (5, {})} | custom-call | flops 1000000000 | bytes 800000 | tf_op jit(solution)/shard_map/second_step/pallas_call | solution.py:186
  91.6 2.4 %second_step.6 = (f32[2,8,256,256]{3,2,1,0:T(8,128)}, f32[2,256,256]{2,1,0:T(8,128)S(1)}, f32[8,128]{1,0:T(8,128)S(1)}) custom-call(f32[2,1,256,256]{3,2,1,0:T(8,128)S(1)} %collective-permute-done.10.s_ref, f32[8,256,256]{2,1,0:T(8,128)S(1)} %bitcast.55, ...), custom_call_target="tpu_custom_call", output_to_operand_aliasing={{1}: (4, {}), {2}: (5, {}), {0}: (6, {})} | custom-call | flops 1000000000 | bytes 400000 | tf_op jit(solution)/shard_map/second_step/pallas_call | solution.py:186
  94.0 4.2 %second_step.7 = (f32[2,8,256,256]{3,2,1,0:T(8,128)}, f32[2,256,256]{2,1,0:T(8,128)S(1)}, f32[8,128]{1,0:T(8,128)S(1)}) custom-call(f32[2,2,256,256]{3,2,1,0:T(8,128)S(1)} %collective-permute-done.9.s_ref, f32[8,256,256]{2,1,0:T(8,128)S(1)} %bitcast.56, ...), custom_call_target="tpu_custom_call", output_to_operand_aliasing={{1}: (4, {}), {2}: (5, {}), {0}: (6, {})} | custom-call | flops 1000000000 | bytes 800000 | tf_op jit(solution)/shard_map/second_step/pallas_call | solution.py:186
  98.1 3.5 %collective-permute-done.7.s_ref = f32[2,1,256,256]{3,2,1,0:T(8,128)S(1)} collective-permute-done((f32[2,1,256,256]{3,2,1,0:T(8,128)S(1)}, f32[2,1,256,256]{3,2,1,0:T(8,128)S(1)}, u32[]{:S(2)}, u32[]{:S(2)}) %collective-permute-start.7) | collective-permute-done | bytes 524320 | tf_op jit(solution)/shard_map/ppermute | solution.py:274
  101.7 2.4 %second_step.8 = (f32[2,8,256,256]{3,2,1,0:T(8,128)}, f32[2,256,256]{2,1,0:T(8,128)S(1)}, f32[8,128]{1,0:T(8,128)S(1)}) custom-call(f32[2,1,256,256]{3,2,1,0:T(8,128)S(1)} %collective-permute-done.7.s_ref, f32[8,256,256]{2,1,0:T(8,128)S(1)} %bitcast.57, ...), custom_call_target="tpu_custom_call", output_to_operand_aliasing={{1}: (4, {}), {2}: (5, {}), {0}: (6, {})} | custom-call | flops 20000000000 | bytes 400000 | tf_op jit(solution)/shard_map/second_step/pallas_call | solution.py:186
  104.1 3.0 %collective-permute-done.4.s_ref = f32[2,1,256,256]{3,2,1,0:T(8,128)S(1)} collective-permute-done((f32[2,1,256,256]{3,2,1,0:T(8,128)S(1)}, f32[2,1,256,256]{3,2,1,0:T(8,128)S(1)}, u32[]{:S(2)}, u32[]{:S(2)}) %collective-permute-start.4) | collective-permute-done | bytes 524320 | tf_op jit(solution)/shard_map/ppermute | solution.py:274
  107.1 5.8 %collective-permute-done.12.other_ref = f32[2,1,256,256]{3,2,1,0:T(8,128)S(1)} collective-permute-done((f32[2,1,256,256]{3,2,1,0:T(8,128)S(1)}, f32[2,1,256,256]{3,2,1,0:T(8,128)S(1)}, u32[]{:S(2)}, u32[]{:S(2)}) %collective-permute-start.12) | collective-permute-done | bytes 524320 | tf_op jit(solution)/shard_map/ppermute | solution.py:274
  112.9 4.1 %second_step.9 = (f32[2,8,256,256]{3,2,1,0:T(8,128)}, f32[2,256,256]{2,1,0:T(8,128)S(1)}, f32[8,128]{1,0:T(8,128)S(1)}) custom-call(f32[2,1,256,256]{3,2,1,0:T(8,128)S(1)} %collective-permute-done.4.s_ref, f32[8,256,256]{2,1,0:T(8,128)S(1)} %bitcast.58, ...), custom_call_target="tpu_custom_call", output_to_operand_aliasing={{1}: (4, {}), {2}: (6, {}), {0}: (7, {})} | custom-call | flops 1000000000 | bytes 800000 | tf_op jit(solution)/shard_map/second_step/pallas_call | solution.py:206
  117.0 0.9 finish.1
  118.0 22.6 %all_to_all.11 = f32[128,8,128]{2,1,0:T(8,128)S(1)} all-to-all(f32[128,8,128]{2,1,0:T(8,128)S(1)} %bitcast.59), channel_id=1, replica_groups=mesh['tile'=16,'plane'=8] {'tile','plane'}, dimensions={0} | all-to-all | bytes 1048576 | tf_op jit(solution)/shard_map/all_to_all | solution.py:254
  140.5 0.1 reduce_sum.9
  140.7 17.8 %all_to_all.10 = f32[128,8,128]{2,1,0:T(8,128)S(1)} all-to-all(f32[128,8,128]{2,1,0:T(8,128)S(1)} %broadcast_in_dim.14), channel_id=1, replica_groups=mesh['tile'=16,'plane'=8] {'tile','plane'}, dimensions={0} | all-to-all | bytes 1048576 | tf_op jit(solution)/shard_map/all_to_all | solution.py:256
  158.5 0.2 copy.40
  158.7 1.0 copy.42
  (22 shorter events, 0.3 us)
Async XLA Ops:
  0.6 7.8 %copy-start = (f32[2,256,256]{2,1,0:T(8,128)S(1)}, f32[2,256,256]{2,1,0:T(8,128)}, u32[]{:S(2)}) copy-start(f32[2,256,256]{2,1,0:T(8,128)} %param.12) | copy-start | bytes 1572868
  0.6 9.5 %copy-start.5 = (f32[256,256,1]{1,0,2:T(8,128)S(1)}, f32[256,256,1]{1,0,2:T(8,128)}, u32[]{:S(2)}) copy-start(f32[256,256,1]{1,0,2:T(8,128)} %constant.21) | copy-start | bytes 786436
  0.7 10.8 %copy-start.6 = (f32[256,256]{1,0:T(8,128)S(1)}, f32[256,256]{1,0:T(8,128)}, u32[]{:S(2)}) copy-start(f32[256,256]{1,0:T(8,128)} %constant.16.clone) | copy-start | bytes 786436
  0.7 10.8 %collective-permute-start = (f32[1]{0:T(128)}, f32[1]{0:T(128)}, u32[]{:S(2)}, u32[]{:S(2)}) collective-permute-start(f32[1]{0:T(128)} %param.13), channel_id=1, source_target_pairs={{0,1},{1,2},{2,3},{3,4},{4,5},{5,6},{6,7},{7,0},{8,9},{9,10},{10,1... | collective-permute-start | bytes 20 | tf_op jit(solution)/shard_map/ppermute | solution.py:274
  3.9 14.0 %collective-permute-start.2 = (f32[2,256,256]{2,1,0:T(8,128)S(1)}, f32[2,256,256]{2,1,0:T(8,128)S(1)}, u32[]{:S(2)}, u32[]{:S(2)}) collective-permute-start(f32[2,256,256]{2,1,0:T(8,128)S(1)} %slice_bitcast_fusion), channel_id=1, source_target_pairs={{0,7},{1,0},{2,1},{3,2},{4,3},{5,4},{6,5},{7,6},{8,15},{9,8},{10,9... | collective-permute-start | bytes 1572872 | tf_op jit(solution)/shard_map/ppermute | solution.py:274
  6.9 7.4 %copy-start.1 = (f32[1,8,256,256]{3,2,1,0:T(8,128)S(1)}, f32[1,8,256,256]{3,2,1,0:T(8,128)}, u32[]{:S(2)}) copy-start(f32[1,8,256,256]{3,2,1,0:T(8,128)} %param.11) | copy-start | bytes 6291460
  8.3 9.4 %copy-start.3 = (f32[2,1,8,256,256]{4,3,2,1,0:T(8,128)S(1)}, f32[2,1,8,256,256]{4,3,2,1,0:T(8,128)}, u32[]{:S(2)}) copy-start(f32[2,1,8,256,256]{4,3,2,1,0:T(8,128)} %param.10) | copy-start | bytes 12582916
  8.4 26.4 %collective-permute-start.6 = (f32[2,2,256,256]{3,2,1,0:T(8,128)S(1)}, f32[2,2,256,256]{3,2,1,0:T(8,128)S(1)}, u32[]{:S(2)}, u32[]{:S(2)}) collective-permute-start(f32[2,2,256,256]{3,2,1,0:T(8,128)S(1)} %slice.32), channel_id=1, source_target_pairs={{0,1},{1,2},{2,3},{3,4},{4,5},{5,6},{6,7},{7,0},{8,9},{9,10},{10,1... | collective-permute-start | bytes 3145736 | tf_op jit(solution)/shard_map/ppermute | solution.py:274
  11.5 6.6 %copy-start.2 = (bf16[2,4,256,256]{3,2,1,0:T(8,128)(2,1)S(1)}, bf16[2,4,256,256]{3,2,1,0:T(8,128)(2,1)}, u32[]{:S(2)}) copy-start(bf16[2,4,256,256]{3,2,1,0:T(8,128)(2,1)} %constant.4.clone.tables) | copy-start | bytes 3145732
  14.3 14.2 %collective-permute-start.1 = (f32[2,256,256]{2,1,0:T(8,128)S(1)}, f32[2,256,256]{2,1,0:T(8,128)S(1)}, u32[]{:S(2)}, u32[]{:S(2)}) collective-permute-start(f32[2,256,256]{2,1,0:T(8,128)S(1)} %slice.25), channel_id=1, source_target_pairs={{0,7},{1,0},{2,1},{3,2},{4,3},{5,4},{6,5},{7,6},{8,15},{9,8},{10,9... | collective-permute-start | bytes 1572872 | tf_op jit(solution)/shard_map/ppermute | solution.py:274
  17.9 39.2 %collective-permute-start.5 = (f32[2,2,256,256]{3,2,1,0:T(8,128)S(1)}, f32[2,2,256,256]{3,2,1,0:T(8,128)S(1)}, u32[]{:S(2)}, u32[]{:S(2)}) collective-permute-start(f32[2,2,256,256]{3,2,1,0:T(8,128)S(1)} %slice.28), channel_id=1, source_target_pairs={{0,1},{1,2},{2,3},{3,4},{4,5},{5,6},{6,7},{7,0},{8,9},{9,10},{10,1... | collective-permute-start | bytes 3145736 | tf_op jit(solution)/shard_map/ppermute | solution.py:274
  23.1 27.9 %collective-permute-start.8 = (f32[2,2,256,256]{3,2,1,0:T(8,128)S(1)}, f32[2,2,256,256]{3,2,1,0:T(8,128)S(1)}, u32[]{:S(2)}, u32[]{:S(2)}) collective-permute-start(f32[2,2,256,256]{3,2,1,0:T(8,128)S(1)} %get-tuple-element.49), channel_id=1, source_target_pairs={{0,3},{1,0},{2,5},{3,6},{4,7},{5,4},{6,1},{7,2},{8,11},{9,8},{10,1... | collective-permute-start | bytes 3145736 | tf_op jit(solution)/shard_map/ppermute | solution.py:274
  30.8 31.5 %collective-permute-start.3 = (f32[2,1,256,256]{3,2,1,0:T(8,128)S(1)}, f32[2,1,256,256]{3,2,1,0:T(8,128)S(1)}, u32[]{:S(2)}, u32[]{:S(2)}) collective-permute-start(f32[2,1,256,256]{3,2,1,0:T(8,128)S(1)} %get-tuple-element.40), channel_id=1, source_target_pairs={{0,3},{1,0},{2,5},{3,6},{4,7},{5,4},{6,1},{7,2},{8,11},{9,8},{10,1... | collective-permute-start | bytes 1572872 | tf_op jit(solution)/shard_map/ppermute | solution.py:274
  39.8 40.7 %collective-permute-start.11 = (f32[2,2,256,256]{3,2,1,0:T(8,128)S(1)}, f32[2,2,256,256]{3,2,1,0:T(8,128)S(1)}, u32[]{:S(2)}, u32[]{:S(2)}) collective-permute-start(f32[2,2,256,256]{3,2,1,0:T(8,128)S(1)} %get-tuple-element.51), channel_id=1, source_target_pairs={{0,1},{1,2},{2,3},{3,4},{4,5},{5,6},{6,7},{7,0},{8,9},{9,10},{10,1... | collective-permute-start | bytes 3145736 | tf_op jit(solution)/shard_map/ppermute | solution.py:274
  50.9 43.0 %collective-permute-start.9 = (f32[2,2,256,256]{3,2,1,0:T(8,128)S(1)}, f32[2,2,256,256]{3,2,1,0:T(8,128)S(1)}, u32[]{:S(2)}, u32[]{:S(2)}) collective-permute-start(f32[2,2,256,256]{3,2,1,0:T(8,128)S(1)} %collective-permute-done.8), channel_id=1, source_target_pairs={{3,2},{0,3},{5,4},{6,5},{7,6},{4,7},{1,0},{2,1},{11,10},{8,11},{13... | collective-permute-start | bytes 3145736 | tf_op jit(solution)/shard_map/ppermute | solution.py:274
  56.7 34.8 %collective-permute-start.10 = (f32[2,1,256,256]{3,2,1,0:T(8,128)S(1)}, f32[2,1,256,256]{3,2,1,0:T(8,128)S(1)}, u32[]{:S(2)}, u32[]{:S(2)}) collective-permute-start(f32[2,1,256,256]{3,2,1,0:T(8,128)S(1)} %get-tuple-element.50), channel_id=1, source_target_pairs={{0,2},{1,3},{2,4},{3,5},{4,6},{5,7},{6,0},{7,1},{8,10},{9,11},{10,... | collective-permute-start | bytes 1572872 | tf_op jit(solution)/shard_map/ppermute | solution.py:274
  59.5 42.2 %collective-permute-start.7 = (f32[2,1,256,256]{3,2,1,0:T(8,128)S(1)}, f32[2,1,256,256]{3,2,1,0:T(8,128)S(1)}, u32[]{:S(2)}, u32[]{:S(2)}) collective-permute-start(f32[2,1,256,256]{3,2,1,0:T(8,128)S(1)} %get-tuple-element.48), channel_id=1, source_target_pairs={{0,1},{1,2},{2,3},{3,4},{4,5},{5,6},{6,7},{7,0},{8,9},{9,10},{10,1... | collective-permute-start | bytes 1572872 | tf_op jit(solution)/shard_map/ppermute | solution.py:274
  62.3 50.5 %collective-permute-start.12 = (f32[2,1,256,256]{3,2,1,0:T(8,128)S(1)}, f32[2,1,256,256]{3,2,1,0:T(8,128)S(1)}, u32[]{:S(2)}, u32[]{:S(2)}) collective-permute-start(f32[2,1,256,256]{3,2,1,0:T(8,128)S(1)} %get-tuple-element.66), channel_id=1, source_target_pairs={{0,1},{1,2},{2,3},{3,4},{4,5},{5,6},{6,7},{7,0},{8,9},{9,10},{10,1... | collective-permute-start | bytes 1572872 | tf_op jit(solution)/shard_map/ppermute | solution.py:274
  80.5 26.6 %collective-permute-start.4 = (f32[2,1,256,256]{3,2,1,0:T(8,128)S(1)}, f32[2,1,256,256]{3,2,1,0:T(8,128)S(1)}, u32[]{:S(2)}, u32[]{:S(2)}) collective-permute-start(f32[2,1,256,256]{3,2,1,0:T(8,128)S(1)} %collective-permute-done.3), channel_id=1, source_target_pairs={{3,2},{0,3},{5,4},{6,5},{7,6},{4,7},{1,0},{2,1},{11,10},{8,11},{13... | collective-permute-start | bytes 1572872 | tf_op jit(solution)/shard_map/ppermute | solution.py:274
  112.9 4.1 %copy-start.4 = (bf16[2,256,256]{2,1,0:T(8,128)(2,1)S(1)}, bf16[2,256,256]{2,1,0:T(8,128)(2,1)}, u32[]{:S(2)}) copy-start(bf16[2,256,256]{2,1,0:T(8,128)(2,1)} %constant.17.clone.mix) | copy-start | bytes 786436
